TPU v7x, 32 devices: a whole 2x2x4 slice. The times are simulated.
32 devices in a mesh: seq: 8 (over z, y), tp: 4 (over x, core).
Axes of the slice: x: 2, y: 2, z: 4, core: 2. Of those that a mesh axis runs over, the one named last changes fastest.
Arguments:
- hidden: bfloat16 [8192, 2048], P('seq', 'tp'), may hold values from -6 to 6
- x_weight: bfloat16 [2048, 4096], P(None, 'tp'), may hold values from -0.125 to 0.125
- z_weight: bfloat16 [2048, 4096], P(None, 'tp'), may hold values from -0.125 to 0.125
- bc_weight: bfloat16 [2048, 256], P(None, 'tp'), may hold values from -0.125 to 0.125
- dt_weight: bfloat16 [2048, 64], P(None, 'tp'), may hold values from -0.125 to 0.125
- conv_x: float32 [4, 4096], P(None, 'tp'), may hold values from -3 to 3
- conv_bc: float32 [4, 256], replicated, may hold values from -3 to 3
- dt_bias: float32 [64], P('tp'), may hold values from -2 to 1
- decay_rate: float32 [64], P('tp'), may hold values from 2e-05 to 0.2
- skip_gain: float32 [64], P('tp'), may hold values from 0.2 to 1.5
- norm_gain: float32 [4096], P('tp'), may hold values from 0.5 to 1.5
- out_weight: bfloat16 [4096, 2048], P('tp'), may hold values from -0.09375 to 0.09375
- lengths: int32 [4], replicated, may hold values from 1 to 4096, as said below
- owners: int32 [8], P('seq'), may hold values from 0 to 3, as said below
Outputs:
- mixed: bfloat16 [8192, 2048], P('seq', 'tp')
- final_state: float32 [8, 64, 64, 128], P('seq', 'tp')
- conv_edge_x: bfloat16 [8, 3, 4096], P('seq', None, 'tp')
- conv_edge_bc: bfloat16 [8, 3, 256], P('seq')
Inputs may be any that keep to these rules, and one draw needn't show every extreme that they name: The prompts are packed in order and their lengths sum to 8192; the second prompt is the longest and holds exactly half of 8192 tokens; the third and fourth together hold at least 3 tokens, and one of them holds one or two. `owners`: every prompt is kept by the same number of indices.
All inputs are finite; a program needn't handle non-finite values.
Results may differ from a plain program's by a relative error of at most 0.013.
Values may be sent and summed in bfloat16 or wider, within the bound.
A program may use at most 192 MiB of HBM per device.

v0:
```python
import jax
import jax.numpy as jnp
from jax import lax
from jax.sharding import PartitionSpec as P

NS = 128
KCONV = 4
GROUP = 256
PROMPTS = 4
DIN = 4096


highest = lax.Precision.HIGHEST
epsilon = 1e-05


def passed_along(block, axis, distance):
    devices = range(lax.axis_size(axis))
    route = [(i - distance, i) for i in devices if i - distance in devices]
    return lax.ppermute(block, axis, route)


def prefix(value, axis, join, neutral):
    count, mine = (lax.axis_size(axis), lax.axis_index(axis))
    pieces = jax.tree.map(lambda part: lax.all_gather(part, axis), value)
    running = jax.tree.map(
        lambda part, zero: jnp.full_like(part, 0) + jnp.asarray(zero, part.dtype), value, neutral
    )

    def lap(position, running):
        longer = join(running, jax.tree.map(lambda part: part[position], pieces))
        return jax.tree.map(lambda new, old: jnp.where(position < mine, new, old), longer, running)

    return lax.fori_loop(0, count - 1, lap, running)


def segment_of(positions, prompt_end):
    counted = jnp.sum((positions[:, None] >= prompt_end[None, :]).astype(jnp.int32), axis=1)
    return jnp.where(positions < 0, -1, counted)


def short_conv(extended, seg_ext, kernel):
    taps = kernel.shape[0]
    count = extended.shape[0] - taps + 1
    total = jnp.zeros((count, extended.shape[1]), jnp.float32)
    for offset in range(taps):
        same = (seg_ext[offset : offset + count] == seg_ext[taps - 1 :]).astype(jnp.float32)
        total = (
            total
            + extended[offset : offset + count].astype(jnp.float32)
            * kernel[offset][None, :]
            * same[:, None]
        )
    return jax.nn.silu(total).astype(jnp.bfloat16)


def advance_block(state, block):
    x_blk, b_blk, c_blk, dt_blk, log_blk, seg_blk, seg_prior = block
    length = seg_blk.shape[0]
    acum = jnp.cumsum(log_blk, axis=0)
    index = jnp.arange(length, dtype=jnp.int32)
    keep = (seg_blk[:, None] == seg_blk[None, :]) & (index[:, None] >= index[None, :])
    spread = acum[:, None, :] - acum[None, :, :]
    decay = jnp.where(keep[:, :, None], jnp.exp(jnp.where(keep[:, :, None], spread, 0.0)), 0.0)
    scores = jnp.dot(c_blk, b_blk.T, precision=highest)
    mixing = scores[:, :, None] * decay * dt_blk[None, :, :]
    output = jnp.einsum("ijh,jhp->ihp", mixing, x_blk, precision=highest)
    inflow = jnp.where((seg_blk == seg_prior)[:, None], jnp.exp(acum), 0.0)
    output = output + inflow[:, :, None] * jnp.einsum(
        "in,hpn->ihp", c_blk, state, precision=highest
    )
    closing = seg_blk[length - 1]
    tail = (
        jnp.where((seg_blk == closing)[:, None], jnp.exp(acum[length - 1][None, :] - acum), 0.0)
        * dt_blk
    )
    fresh = jnp.einsum("jh,jhp,jn->hpn", tail, x_blk, b_blk, precision=highest)
    carry = jnp.where(closing == seg_prior, jnp.exp(acum[length - 1]), 0.0)
    return (carry[:, None, None] * state + fresh, (output, state))


def state_at(start_state, seg_prior, x_rows, b_rows, dt_rows, log_rows, seg_rows, inner, prompt):
    acum = jnp.cumsum(log_rows, axis=0)
    level = acum[inner]
    index = jnp.arange(seg_rows.shape[0], dtype=jnp.int32)
    chosen = (seg_rows == prompt) & (index <= inner)
    weight = (
        jnp.where(
            chosen[:, None], jnp.exp(jnp.where(chosen[:, None], level[None, :] - acum, 0.0)), 0.0
        )
        * dt_rows
    )
    inflow = jnp.where(seg_rows[inner] == seg_prior, jnp.exp(level), 0.0)
    return inflow[:, None, None] * start_state + jnp.einsum(
        "jh,jhp,jn->hpn", weight, x_rows, b_rows, precision=highest
    )


def per_device(
    hidden,
    x_weight,
    z_weight,
    bc_weight,
    dt_weight,
    conv_x,
    conv_bc,
    dt_bias,
    decay_rate,
    skip_gain,
    norm_gain,
    out_weight,
    lengths,
    owners,
):
    rows_here = hidden.shape[0]
    width_here = x_weight.shape[1]
    heads_here = dt_bias.shape[0]
    head_width = width_here // heads_here
    my_index = lax.axis_index("seq")
    first_row = my_index * rows_here
    prompt_end = jnp.cumsum(lengths)
    prompt_start = prompt_end - lengths
    positions = first_row + jnp.arange(rows_here, dtype=jnp.int32)
    segment = segment_of(positions, prompt_end)
    bc_full = lax.all_gather(bc_weight, "tp", axis=1, tiled=True)
    piece = lax.all_gather(hidden, "tp", axis=1, tiled=True)

    def take(matrix):
        return jnp.dot(piece, matrix, preferred_element_type=jnp.float32)

    x_acc = take(x_weight)
    z_acc = take(z_weight)
    dt_raw = take(dt_weight)
    bc_acc = take(bc_full)
    x_in = x_acc.astype(jnp.bfloat16)
    z_in = z_acc.astype(jnp.bfloat16)
    bc_in = bc_acc.astype(jnp.bfloat16)
    joined = jnp.concatenate([x_in, bc_in], axis=1)
    earlier = passed_along(joined[rows_here - (KCONV - 1) :], "seq", 1)
    extended = jnp.concatenate([earlier, joined], axis=0)
    seg_ext = jnp.concatenate(
        [
            segment_of(
                first_row - (KCONV - 1) + jnp.arange(KCONV - 1, dtype=jnp.int32), prompt_end
            ),
            segment,
        ]
    )
    kernel = jnp.concatenate([conv_x, conv_bc], axis=1)
    mixed_in = short_conv(extended, seg_ext, kernel)
    x_conv = mixed_in[:, :width_here].astype(jnp.float32).reshape(rows_here, heads_here, head_width)
    b_conv = mixed_in[:, width_here : width_here + NS].astype(jnp.float32)
    c_conv = mixed_in[:, width_here + NS :].astype(jnp.float32)
    step_size = jax.nn.softplus(dt_raw + dt_bias[None, :])
    log_decay = -decay_rate[None, :] * step_size
    blocks = rows_here // GROUP
    block_first = first_row + jnp.arange(blocks, dtype=jnp.int32) * GROUP
    seg_prior = segment_of(block_first - 1, prompt_end)
    packed = (
        x_conv.reshape(blocks, GROUP, heads_here, head_width),
        b_conv.reshape(blocks, GROUP, NS),
        c_conv.reshape(blocks, GROUP, NS),
        step_size.reshape(blocks, GROUP, heads_here),
        log_decay.reshape(blocks, GROUP, heads_here),
        segment.reshape(blocks, GROUP),
        seg_prior,
    )
    init_state = jnp.zeros((heads_here, head_width, NS), jnp.float32)
    local_end, (outputs, priors) = lax.scan(advance_block, init_state, packed)
    device_prior = seg_prior[0]
    level = jnp.cumsum(log_decay, axis=0)
    through = jnp.where(segment[rows_here - 1] == device_prior, jnp.exp(level[rows_here - 1]), 0.0)

    def link(earlier_pair, later_pair):
        return (
            earlier_pair[0] * later_pair[0],
            later_pair[0][:, None, None] * earlier_pair[1] + later_pair[1],
        )

    unused, entering = prefix(
        (through, local_end), "seq", link, (jnp.ones_like(through), jnp.zeros_like(local_end))
    )
    inflow = jnp.where((segment == device_prior)[:, None], jnp.exp(level), 0.0)
    ssm = outputs.reshape(rows_here, heads_here, head_width)
    ssm = ssm + inflow[:, :, None] * jnp.einsum("in,hpn->ihp", c_conv, entering, precision=highest)
    ssm = ssm + skip_gain[None, :, None] * x_conv
    gated = ssm.reshape(rows_here, width_here) * jax.nn.silu(z_in.astype(jnp.float32))
    square_sum = lax.psum(jnp.sum(gated * gated, axis=1), "tp")
    normed = (gated * lax.rsqrt(square_sum / DIN + epsilon)[:, None] * norm_gain[None, :]).astype(
        jnp.bfloat16
    )
    mixed_cols = lax.psum_scatter(
        lax.dot_general(
            out_weight, normed, (((0,), (1,)), ((), ())), preferred_element_type=jnp.float32
        ),
        "tp",
        scatter_dimension=0,
        tiled=True,
    )
    mixed = mixed_cols.T.astype(jnp.bfloat16)
    last_row = prompt_end - 1
    holder = last_row // rows_here
    present = holder == my_index
    inner = jnp.clip(last_row - first_row, 0, rows_here - 1)

    def finish(prompt_id, inner_row):
        return state_at(
            entering,
            device_prior,
            x_conv,
            b_conv,
            step_size,
            log_decay,
            segment,
            inner_row,
            prompt_id,
        )

    finals = jax.vmap(finish)(jnp.arange(PROMPTS, dtype=jnp.int32), inner)
    finals = jnp.where(present[:, None, None, None], finals, 0.0)

    def edge_of(inner_row, start_row, end_row):
        window = lax.dynamic_slice_in_dim(extended, inner_row + 1, KCONV - 1, 0)
        rows_global = end_row - (KCONV - 2) + jnp.arange(KCONV - 1, dtype=jnp.int32)
        return jnp.where((rows_global >= start_row)[:, None], window, jnp.zeros_like(window))

    edges = jax.vmap(edge_of)(inner, prompt_start, last_row)
    edges = jnp.where(present[:, None, None], edges.astype(jnp.float32), 0.0)
    finals_all, edges_all = lax.psum((finals, edges), "seq")
    keeper = owners[0]
    final_state = finals_all[keeper][None]
    kept_edges = edges_all[keeper]
    conv_edge_x = kept_edges[:, :width_here].astype(jnp.bfloat16)[None]
    conv_edge_bc = kept_edges[:, width_here:].astype(jnp.bfloat16)[None]
    return (mixed, final_state, conv_edge_x, conv_edge_bc)


def solution(mesh):
    return jax.shard_map(
        per_device,
        mesh=mesh,
        in_specs=(
            P("seq", "tp"),
            P(None, "tp"),
            P(None, "tp"),
            P(None, "tp"),
            P(None, "tp"),
            P(None, "tp"),
            P(),
            P("tp"),
            P("tp"),
            P("tp"),
            P("tp"),
            P("tp", None),
            P(),
            P("seq"),
        ),
        out_specs=(
            P("seq", "tp"),
            P("seq", "tp", None, None),
            P("seq", None, "tp"),
            P("seq", None, None),
        ),
        check_vma=False,
    )
```

profile of v0, /device:TPU:0, one launch (start us, length us, event | category | flops | bytes accessed | tf_op | source)
XLA Modules:
  0.0 549.7 jit_solution(2216654934978029078)
XLA Ops:
  12.4 16.7 %all-gather.8.cloned.1.call-done = bf16[2048,256]{0,1:T(8,128)(2,1)} async-done(((bf16[2048,64]{0,1:T(8,128)(2,1)}), bf16[2048,256]{0,1:T(8,128)(2,1)}) %all-gather.8.cloned.1.call-update) | async-done | bytes 1048592 | tf_op jit(solution)/shard_map/all_gather | solution.py:125
  29.0 36.1 %all-gather.6.cloned.1.call-done = bf16[1024,2048]{1,0:T(8,128)(2,1)} async-done(((bf16[1024,512]{1,0:T(8,128)(2,1)}), bf16[1024,2048]{1,0:T(8,128)(2,1)}) %all-gather.6.cloned.1.call-update) | async-done | bytes 4194320 | tf_op jit(solution)/shard_map/all_gather | solution.py:126
  65.1 3.9 convolution_convert_fusion.1
  69.1 7.0 %convolution_convert_fusion = bf16[1024,1024]{0,1:T(8,128)(2,1)S(1)} fusion(bf16[1024,2048]{1,0:T(8,128)(2,1)S(1)} %copy-done.6, bf16[2048,1024]{1,0:T(8,128)(2,1)} %param.19), kind=kOutput, calls=%fused_computation.87 | convolution fusion | flops 4296015872 | bytes 10485760 | tf_op jit(solution)/shard_map/dot_general | solution.py:129
  76.9 4.1 collective-permute-start
  82.3 5.6 %collective-permute-done = bf16[3,1280]{0,1:T(8,128)(2,1)} collective-permute-done((bf16[3,1280]{0,1:T(8,128)(2,1)}, bf16[3,1280]{0,1:T(8,128)(2,1)}, u32[]{:S(2)}, u32[]{:S(2)}) %collective-permute-start) | collective-permute-done | bytes 7712 | tf_op jit(solution)/shard_map/ppermute | solution.py:20
  90.8 7.4 %multiply_convert_fusion = bf16[1024,1280]{0,1:T(8,128)(2,1)S(1)} fusion(bf16[1024,256]{0,1:T(8,128)(2,1)S(1)} %convolution_convert_fusion.1, bf16[1027,1280]{0,1:T(8,128)(2,1)S(1)} %maximum_maximum_fusion, f32[1280]{0:T(1024)S(1)} %get-tuple-element.304, f32[1024]{0:T(1024)S(1)} %get-tuple-element.360, f32[1280]{0:T(1024)S(1)} %get-tuple-element.305, ...), kind=kLoop, calls=%fused_computation.69 | loop fusion | flops 28835840 | bytes 13139968 | tf_op jit(solution)/shard_map/convert_element_type | solution.py:54
  102.6 5.6 %reshape_reshape.3 = f32[4,256,16,64]{1,0,3,2:T(4,128)} reshape(f32[1024,1024]{0,1:T(8,128)} %slice_convert_fusion) | data formatting | bytes 8388608 | tf_op jit(solution)/shard_map/reshape;reshape | solution.py:160
  108.2 161.4 %while.32 = (s32[]{:T(128)}, f32[16,64,128]{2,1,0:T(8,128)S(1)}, f32[4,256,16,64]{1,0,3,2:T(4,128)}, s32[4,256]{1,0:T(4,128)S(1)}, s32[4]{0:T(128)S(1)}, /*index...) while((s32[]{:T(128)}, f32[16,64,128]{2,1,0:T(8,128)S(1)}, ...), condition=%wide.region_7.8_spmd.clone.clone, body=%wide.region_4.7_spmd.clone.sunk.clone | while | flops 1718571520 | bytes 14622798 | solution.py:169
  117.0 4.9 fusion.121
  125.3 23.4 %dynamic_update_slice.7 = f32[4,256,16,64]{1,0,3,2:T(4,128)} dynamic-update-slice(f32[4,256,16,64]{1,0,3,2:T(4,128)} %get-tuple-element.565, f32[1,256,16,64]{1,0,3,2:T(1,128)S(1)} %copy.168, s32[]{:T(128)S(6)} %copy.175, s32[]{:T(128)} %constant.101.clone.1..sunk.2, s32[]{:T(128)} %constant.101.clone.1..sunk.2, s32[]{:T(128)} %constant.101.clone.1..sunk.2) | dynamic-update-slice | bytes 2097156 | tf_op jit(solution)/shard_map/while/body/jit(dynamic_update_index_in_dim)/dynamic_update_slice | solution.py:169
  157.3 4.9 fusion.121
  165.6 23.4 %dynamic_update_slice.7 = f32[4,256,16,64]{1,0,3,2:T(4,128)} dynamic-update-slice(f32[4,256,16,64]{1,0,3,2:T(4,128)} %get-tuple-element.565, f32[1,256,16,64]{1,0,3,2:T(1,128)S(1)} %copy.168, s32[]{:T(128)S(6)} %copy.175, s32[]{:T(128)} %constant.101.clone.1..sunk.2, s32[]{:T(128)} %constant.101.clone.1..sunk.2, s32[]{:T(128)} %constant.101.clone.1..sunk.2) | dynamic-update-slice | bytes 2097156 | tf_op jit(solution)/shard_map/while/body/jit(dynamic_update_index_in_dim)/dynamic_update_slice | solution.py:169
  197.7 4.9 fusion.121
  205.9 23.4 %dynamic_update_slice.7 = f32[4,256,16,64]{1,0,3,2:T(4,128)} dynamic-update-slice(f32[4,256,16,64]{1,0,3,2:T(4,128)} %get-tuple-element.565, f32[1,256,16,64]{1,0,3,2:T(1,128)S(1)} %copy.168, s32[]{:T(128)S(6)} %copy.175, s32[]{:T(128)} %constant.101.clone.1..sunk.2, s32[]{:T(128)} %constant.101.clone.1..sunk.2, s32[]{:T(128)} %constant.101.clone.1..sunk.2) | dynamic-update-slice | bytes 2097156 | tf_op jit(solution)/shard_map/while/body/jit(dynamic_update_index_in_dim)/dynamic_update_slice | solution.py:169
  238.0 4.9 fusion.121
  246.2 23.4 %dynamic_update_slice.7 = f32[4,256,16,64]{1,0,3,2:T(4,128)} dynamic-update-slice(f32[4,256,16,64]{1,0,3,2:T(4,128)} %get-tuple-element.565, f32[1,256,16,64]{1,0,3,2:T(1,128)S(1)} %copy.168, s32[]{:T(128)S(6)} %copy.175, s32[]{:T(128)} %constant.101.clone.1..sunk.2, s32[]{:T(128)} %constant.101.clone.1..sunk.2, s32[]{:T(128)} %constant.101.clone.1..sunk.2) | dynamic-update-slice | bytes 2097156 | tf_op jit(solution)/shard_map/while/body/jit(dynamic_update_index_in_dim)/dynamic_update_slice | solution.py:169
  272.6 4.5 reduce-window.21
  278.7 21.6 %all-gather.1 = f32[8,1,16]{2,1,0:T(1,128)S(1)} all-gather(f32[1,1,16]{2,1,0:T(1,128)S(1)} %bitcast.252), channel_id=1, replica_groups=mesh['seq'=8,'tp'=4] {'seq'}, dimensions={0}, use_global_device_ids=true | all-gather | bytes 576 | tf_op jit(solution)/shard_map/all_gather | solution.py:25
  300.6 6.0 %reshape.362 = f32[1024,16,64]{0,2,1:T(8,128)} reshape(f32[4,256,16,64]{1,0,3,2:T(4,128)} %get-tuple-element.151) | data formatting | bytes 8388608 | tf_op jit(solution)/shard_map/reshape | solution.py:184
  306.5 38.6 %all-gather.10.cloned.1.call-done = f32[128,64,128]{2,1,0:T(8,128)} async-done(((f32[16,64,128]{2,1,0:T(8,128)}), f32[128,64,128]{2,1,0:T(8,128)}) %all-gather.10.cloned.1.call-update) | async-done | bytes 4194320 | tf_op jit(solution)/shard_map/all_gather | solution.py:25
  345.2 8.5 %while.33 = (s32[]{:T(128)}, f32[16,64,128]{2,1,0:T(8,128)S(1)}, s32[]{:T(128)}, f32[8,16]{1,0:T(8,128)S(1)}, f32[8,16,64,128]{3,2,1,0:T(8,128)}) while((s32[]{:T(128)}, f32[16,64,128]{2,1,0:T(8,128)S(1)}, s32[]{:T(128)}, f32[8,16]{1,0:T(8,128)S(1)}, f32[8,16,64,128]{3,2,1,0:T(8,128)}) %tuple.136), condition=%wide.region_11.12_spmd.clone.clone, body=%wide.region_10.11_spmd.clone.sunk.clone | while | flops 524292 | bytes 1573153 | solution.py:34
  353.7 11.7 %fusion.47 = f32[4,16,64,128]{3,2,0,1:T(8,128)} fusion(f32[1024,16,64]{0,2,1:T(8,128)} %bitcast.233, f32[1024,16,4]{0,2,1:T(4,128)S(1)} %multiply_bitcast_fusion, f32[16,64,128]{2,1,0:T(8,128)S(1)} %get-tuple-element.153, f32[4,16]{0,1:T(8,128)S(1)} %copy.101, pred[4]{0:T(512)(128)(4,1)S(1)} %fusion.76, bf16[1024,1280]{0,1:T(8,128)(2,1)} %copy-done.5), kind=kOutput, calls=%fused_computation.84 | convolution fusion | flops 6448218112 | bytes 7340292 | tf_op jit(solution)/shard_map/vmap(jh,jhp,jn->hpn)/dot_general | solution.py:94
  365.5 5.9 %multiply_add_fusion = f32[1024,16,64]{0,2,1:T(8,128)S(1)} fusion(f32[1024,16,64]{0,2,1:T(8,128)} %bitcast.234, f32[1024,16,64]{0,2,1:T(8,128)} %reshape.362, f32[16,64,128]{2,1,0:T(8,128)S(1)} %get-tuple-element.153, f32[16]{0:T(128)S(1)} %copy-done.11, f32[1024,16]{0,1:T(8,128)S(1)} %exponential_select_fusion.1, bf16[1024,1280]{0,1:T(8,128)(2,1)} %copy-done.5), kind=kOutput, calls=%fused_computation.77 | convolution fusion | flops 1614807040 | bytes 13434944 | tf_op jit(solution)/shard_map/in,hpn->ihp/dot_general | solution.py:185
  372.0 7.5 %multiply_reduce_fusion = (f32[1024]{0:T(1024)S(1)}, f32[1024,1024]{0,1:T(8,128)}) fusion(bf16[1024,2048]{1,0:T(8,128)(2,1)S(1)} %copy-done.7, bf16[2048,1024]{1,0:T(8,128)(2,1)S(1)} %copy-done.12, f32[1024,16,64]{0,2,1:T(8,128)S(1)} %multiply_add_fusion), kind=kOutput, calls=%fused_computation.76 | convolution fusion | flops 4304403456 | bytes 16781312 | tf_op jit(solution)/shard_map/dot_general | solution.py:129
  379.5 6.0 %psum.21 = f32[1024]{0:T(1024)S(1)} all-reduce(f32[1024]{0:T(1024)S(1)} %get-tuple-element.368), channel_id=1, replica_groups=mesh['seq'=8,'tp'=4] {'tp'}, use_global_device_ids=true, to_apply=%region_13.14 | all-reduce | flops 1024 | bytes 8192 | tf_op jit(solution)/shard_map/psum | solution.py:188
  385.5 11.5 %convolution_bitcast_fusion = f32[2048,1024]{0,1:T(8,128)} fusion(bf16[1024,2048]{1,0:T(8,128)(2,1)} %param.29, f32[1024,1024]{0,1:T(8,128)} %get-tuple-element.369, f32[1024]{0:T(1024)S(1)} %copy-done.8, f32[1024]{0:T(1024)S(1)} %add_rsqrt_fusion), kind=kOutput, calls=%fused_computation.70 | convolution fusion | flops 4298113024 | bytes 16785408 | tf_op jit(solution)/shard_map/dot_general | solution.py:193
  398.8 3.4 copy.104
  402.2 8.0 %while.31 = (s32[]{:T(128)}, bf16[1027,1280]{1,0:T(8,128)(2,1)}, s32[4,2]{0,1:T(2,128)S(1)}, bf16[4,3,1280]{2,1,0:T(4,128)(2,1)S(1)}) while((s32[]{:T(128)}, bf16[1027,1280]{1,0:T(8,128)(2,1)}, s32[4,2]{0,1:T(2,128)S(1)}, bf16[4,3,1280]{2,1,0:T(4,128)(2,1)S(1)}) %tuple.120), condition=%wide.while_cond.clone, body=%wide.while_body.sunk.clone | while | flops 2 | bytes 18017 | solution.py:223
  410.3 36.5 %psum.23 = bf16[4,3,1280]{2,1,0:T(4,128)(2,1)S(1)} all-reduce(f32[4,3,1280]{2,1,0:T(4,128)S(1)} %convert_select_fusion), channel_id=1, replica_groups=mesh['seq'=8,'tp'=4] {'seq'}, use_global_device_ids=true, to_apply=%region_16.17 | all-reduce | flops 15360 | bytes 92160 | tf_op jit(solution)/shard_map/psum | solution.py:229
  448.0 18.0 %all-reduce.4.cloned.1.call-done = f32[4,16,64,128]{3,2,0,1:T(8,128)} async-done(((f32[4,16,64,128]{3,2,0,1:T(8,128)}), f32[4,16,64,128]{3,2,0,1:T(8,128)}) %all-reduce.4.cloned.1.call-update) | async-done | bytes 2097168 | tf_op jit(solution)/shard_map/psum | solution.py:229
  467.9 72.1 %reduce-scatter.2.cloned.1.call-done = f32[512,1024]{0,1:T(8,128)} async-done(((f32[2048,1024]{0,1:T(8,128)}), f32[512,1024]{0,1:T(8,128)}) %reduce-scatter.2.cloned.1.call-update) | async-done | bytes 2097168 | tf_op jit(solution)/shard_map/reduce_scatter | solution.py:192
  (211 shorter events, 84.8 us)
Async XLA Ops:
  7.2 73.9 %copy-start = (bf16[2048,16]{0,1:T(8,128)(2,1)S(1)}, bf16[2048,16]{0,1:T(8,128)(2,1)}, u32[]{:S(2)}) copy-start(bf16[2048,16]{0,1:T(8,128)(2,1)} %param.22) | copy-start | bytes 196612
  7.2 21.9 %all-gather.8.cloned.1.call-start = ((), (), s32[]{:S(2)}) async-start(), calls=%async_computation.2 | async-start | bytes 1310720 | tf_op jit(solution)/shard_map/all_gather | solution.py:125
  7.9 57.2 %all-gather.6.cloned.1.call-start = ((), (), s32[]{:S(2)}) async-start(), calls=%async_computation.1 | async-start | bytes 5242880 | tf_op jit(solution)/shard_map/all_gather | solution.py:126
  8.7 336.5 %all-gather.10.cloned.1.call-start = ((), (), s32[]{:S(2)}) async-start(), calls=%async_computation.5 | async-start | bytes 4718592 | tf_op jit(solution)/shard_map/all_gather | solution.py:25
  65.1 3.9 copy-start.6
  69.1 12.0 %copy-start.9 = (f32[16]{0:T(128)S(1)}, f32[16]{0:T(128)}, u32[]{:S(2)}) copy-start(f32[16]{0:T(128)} %param.25) | copy-start | bytes 196
  76.9 11.1 %collective-permute-start = (bf16[3,1280]{0,1:T(8,128)(2,1)}, bf16[3,1280]{0,1:T(8,128)(2,1)}, u32[]{:S(2)}, u32[]{:S(2)}) collective-permute-start(bf16[3,1280]{0,1:T(8,128)(2,1)} %fusion.52), channel_id=1, source_target_pairs={{0,4},{4,8},{8,12},{12,16},{16,20},{20,24},{24,28},{1,5},{5,9},{9,... | collective-permute-start | bytes 23048 | tf_op jit(solution)/shard_map/ppermute | solution.py:20
  90.8 7.4 %copy-start.2 = (bf16[1027,1280]{0,1:T(8,128)(2,1)}, bf16[1027,1280]{0,1:T(8,128)(2,1)S(1)}, u32[]{:S(2)}) copy-start(bf16[1027,1280]{0,1:T(8,128)(2,1)S(1)} %maximum_maximum_fusion) | copy-start | bytes 7887364
  98.2 1.6 copy-start.5
  108.2 164.2 %copy-start.10 = (s32[4]{0:T(128)S(1)}, s32[4]{0:T(128)}, u32[]{:S(2)}) copy-start(s32[4]{0:T(128)} %param.30) | copy-start | bytes 52
  269.6 0.8 copy-start.4
  270.5 195.6 %all-reduce.4.cloned.1.call-start = ((), (), s32[]{:S(2)}) async-start(), calls=%async_computation.4 | async-start | bytes 4194304 | tf_op jit(solution)/shard_map/psum | solution.py:229
  353.7 11.8 %copy-start.11 = (f32[16]{0:T(128)S(1)}, f32[16]{0:T(128)}, u32[]{:S(2)}) copy-start(f32[16]{0:T(128)} %param.27) | copy-start | bytes 196
  365.4 174.6 %reduce-scatter.2.cloned.1.call-start = ((), (), s32[]{:S(2)}) async-start(), calls=%async_computation.3 | async-start | bytes 10485760 | tf_op jit(solution)/shard_map/reduce_scatter | solution.py:192
  365.5 6.0 %copy-start.7 = (bf16[1024,2048]{1,0:T(8,128)(2,1)S(1)}, bf16[1024,2048]{1,0:T(8,128)(2,1)}, u32[]{:S(2)}) copy-start(bf16[1024,2048]{1,0:T(8,128)(2,1)} %all-gather.6.cloned.1.call-done) | copy-start | bytes 12582916
  365.5 6.5 %copy-start.12 = (bf16[2048,1024]{1,0:T(8,128)(2,1)S(1)}, bf16[2048,1024]{1,0:T(8,128)(2,1)}, u32[]{:S(2)}) copy-start(bf16[2048,1024]{1,0:T(8,128)(2,1)} %param.20) | copy-start | bytes 12582916
  372.0 13.6 %copy-start.8 = (f32[1024]{0:T(1024)S(1)}, f32[1024]{0:T(1024)}, u32[]{:S(2)}) copy-start(f32[1024]{0:T(1024)} %param.28) | copy-start | bytes 12292
  397.0 1.8 copy-start.3
  397.8 144.9 %copy-start.1 = (bf16[2048,16]{0,1:T(8,128)(2,1)S(1)}, bf16[2048,16]{0,1:T(8,128)(2,1)}, u32[]{:S(2)}) copy-start(bf16[2048,16]{0,1:T(8,128)(2,1)} %param.22) | copy-start | bytes 196612
Sparse Core Ops, SparseCore 0:
  9.6 19.4 all-gather.7
  30.6 34.4 all-gather.5
  270.6 74.5 all-gather.9
  365.5 100.4 all-reduce.3
  468.4 71.5 reduce-scatter.1
where the time goes:
time: 561 us; the launch traced here: 550 us
  waiting for transfers between devices  189 us (34%)
  local copies, waits for them, and re-layouts  152 us (27%)
  matrix products  78.8 us (14%)
  blocking collectives  64.1 us (11%)
  other arithmetic  40.6 us (7%)
  between operations  16 us (3%)
  loops' own time  5.67 us (1%)
    dynamic_update_slice x8, local copies, waits for them, and re-layouts, per_device(): local_end, (outputs, priors) = lax.scan(advance_block, init_state, packed)  98 us
    reduce_scatter x1, waiting for transfers between devices, per_device(): lax.psum_scatter(lax.dot_general(out_weight, normed, (((0,), (1,)), ((),...  72.1 us
    all_gather x1, waiting for transfers between devices, prefix(): pieces = jax.tree.map(lambda part: lax.all_gather(part, axis), value)  38.6 us
    psum x1, blocking collectives, per_device(): finals_all, edges_all = lax.psum((finals, edges), 'seq')  36.5 us
    all_gather x1, waiting for transfers between devices, per_device(): piece = lax.all_gather(hidden, 'tp', axis=1, tiled=True)  36.1 us
    all_gather x1, blocking collectives, prefix(): pieces = jax.tree.map(lambda part: lax.all_gather(part, axis), value)  21.6 us
    dot_general x4, matrix products, advance_block(): output = jnp.einsum('ijh,jhp->ihp', mixing, x_blk, precision=highest)  19.7 us
    dot_general x4, matrix products, take(): return jnp.dot(piece, matrix, preferred_element_type=jnp.float32)  19.6 us
  transfers between devices with their start and end apart: 6, of which 6 were waited for; matrix products, arithmetic and copies ran while one was open for 11% of the time, Pallas kernels for 0%

commit v1 on v0

v1 whole, which is shorter than its diff:
```python
import functools

import jax
import jax.numpy as jnp
from jax import lax
from jax.experimental import pallas as pl
from jax.experimental.pallas import tpu as pltpu
from jax.sharding import PartitionSpec as P

NS = 128
KCONV = 4
PROMPTS = 4
DIN = 4096
CHUNK = 128
LANES = 128
HALO = 16
EXTRA = 16
NEVER = -1e30

epsilon = 1e-05
f32 = jnp.float32
bf16 = jnp.bfloat16


def rows_iota(rows, columns=LANES):
    return lax.broadcasted_iota(jnp.int32, (rows, columns), 0)


def start_of(position, place_ref):
    start = jnp.zeros_like(position)
    for r in range(PROMPTS):
        start = jnp.where(position >= place_ref[r], place_ref[r], start)
    return start


def split(value):
    high = value.astype(bf16)
    return high, (value - high.astype(f32)).astype(bf16)


def spread_heads(value, expand_ref):
    high, low = split(value)
    return jnp.dot(
        jnp.concatenate([high, low], axis=1), expand_ref[...], preferred_element_type=f32
    )


def spread_row(row, expand_ref):
    return spread_heads(jnp.broadcast_to(row, (16, LANES)), expand_ref)[0:1]


def split_rows(row, first, expand_ref):
    high, low = split(jnp.broadcast_to(row, (EXTRA, LANES)))
    at = rows_iota(EXTRA)
    both = jnp.where(at == first, high.astype(f32), 0.0) + jnp.where(
        at == first + 1, low.astype(f32), 0.0
    )
    return jnp.dot(both.astype(bf16), expand_ref[0:LANES], preferred_element_type=f32)


def conv_columns(ext_ref, taps_ref, columns, age):
    total = ext_ref[HALO : HALO + CHUNK, columns] * taps_ref[KCONV - 1 : KCONV, columns]
    for back in range(1, KCONV):
        term = (
            ext_ref[HALO - back : HALO - back + CHUNK, columns]
            * taps_ref[KCONV - 1 - back : KCONV - back, columns]
        )
        total = total + jnp.where(age >= back, term, 0.0)
    return (total * jax.nn.sigmoid(total)).astype(bf16)


def states_kernel(
    place_ref, x_ref, bc_ref, halo_x_ref, halo_bc_ref, dt_ref, taps_x_ref, taps_bc_ref,
    bias_ref, rate_ref, expand_ref,
    xc_ref, xdt_ref, bcc_ref, acum_ref, prior_ref, thr_ref, end_ref, finals_ref,
    ext_x, ext_bc, state, through,
):
    step = pl.program_id(0)
    width = x_ref.shape[1]

    @pl.when(step == 0)
    def _():
        ext_x[0:HALO] = halo_x_ref[...].astype(f32)
        ext_bc[0:HALO] = halo_bc_ref[...].astype(f32)
        state[...] = jnp.zeros_like(state)
        through[...] = jnp.ones_like(through)
        finals_ref[...] = jnp.zeros_like(finals_ref)

    @pl.when(step > 0)
    def _():
        ext_x[0:HALO] = ext_x[CHUNK : CHUNK + HALO]
        ext_bc[0:HALO] = ext_bc[CHUNK : CHUNK + HALO]

    ext_x[HALO : HALO + CHUNK] = x_ref[...].astype(f32)
    ext_bc[HALO : HALO + CHUNK] = bc_ref[...].astype(f32)

    first = place_ref[2 * PROMPTS] + step * CHUNK
    local = rows_iota(CHUNK)
    token = first + local
    age = token - start_of(token, place_ref)
    for tile in range(width // LANES):
        columns = slice(tile * LANES, (tile + 1) * LANES)
        xc_ref[:, columns] = conv_columns(ext_x, taps_x_ref, columns, age)
    for tile in range(2 * NS // LANES):
        columns = slice(tile * LANES, (tile + 1) * LANES)
        bcc_ref[:, columns] = conv_columns(ext_bc, taps_bc_ref, columns, age)

    raw = dt_ref[...] + bias_ref[0:1]
    dt = jnp.maximum(raw, 0.0) + jnp.log1p(jnp.exp(-jnp.abs(raw)))
    log_decay = -rate_ref[0:1] * dt
    lower = (
        local >= lax.broadcasted_iota(jnp.int32, (CHUNK, CHUNK), 1)
    ).astype(f32)
    acum = jnp.dot(
        lower, log_decay, precision=lax.Precision.HIGHEST, preferred_element_type=f32
    )
    acum_ref[...] = acum
    x_dt = xc_ref[...].astype(f32) * spread_heads(dt, expand_ref)
    xdt_ref[...] = x_dt.astype(bf16)
    b_turned = jnp.transpose(bcc_ref[:, 0:NS].astype(f32)).astype(bf16)
    prior_ref[0] = state[...].astype(bf16)
    thr_ref[0] = through[...]

    for r in range(PROMPTS):
        inner = place_ref[r] - 1 - first
        begin = place_ref[PROMPTS + r]

        @pl.when((inner >= 0) & (inner < CHUNK))
        def _():
            level = jnp.sum(jnp.where(local == inner, acum, 0.0), axis=0, keepdims=True)
            chosen = (local <= inner) & (token >= begin)
            weight = jnp.exp(jnp.where(chosen, level - acum, NEVER))
            enter = jnp.exp(level) * (begin < first).astype(f32)
            rows = (x_dt * spread_heads(weight, expand_ref)).astype(bf16)
            finals_ref[r, 0:NS] = (
                spread_row(enter, expand_ref) * state[...]
                + jnp.dot(b_turned, rows, preferred_element_type=f32)
            ).astype(bf16)
            at = rows_iota(EXTRA, HALO + CHUNK)
            place = lax.broadcasted_iota(jnp.int32, (EXTRA, HALO + CHUNK), 1)
            count = KCONV - 1

            def pick(skip):
                wanted = inner - (count - 1) + at - skip
                ok = (at >= skip) & (at < skip + count) & (first + wanted >= begin)
                return jnp.where(ok & (place == HALO + wanted), 1.0, 0.0).astype(bf16)

            edge_x = jnp.dot(pick(0), ext_x[...].astype(bf16), preferred_element_type=f32)
            edge_bc = jnp.dot(pick(count), ext_bc[...].astype(bf16), preferred_element_type=f32)
            edge_bc = jnp.concatenate(
                [edge_bc, jnp.zeros((EXTRA, width - 2 * NS), f32)], axis=1
            )
            passing = split_rows(through[0:1] * enter, 2 * count, expand_ref)
            finals_ref[r, NS : NS + EXTRA] = (edge_x + edge_bc + passing).astype(bf16)

    last = acum[CHUNK - 1 : CHUNK]
    closing = start_of(first + CHUNK - 1, place_ref)
    tail = jnp.exp(jnp.where(token >= closing, last - acum, NEVER))
    carry = jnp.exp(last) * (closing < first).astype(f32)
    rows = (x_dt * spread_heads(tail, expand_ref)).astype(bf16)
    state[...] = spread_row(carry, expand_ref) * state[...] + jnp.dot(
        b_turned, rows, preferred_element_type=f32
    )
    through[...] = through[...] * carry

    @pl.when(step == pl.num_programs(0) - 1)
    def _():
        end_ref[0:NS] = state[...].astype(bf16)
        end_ref[NS : NS + EXTRA] = split_rows(through[0:1], 0, expand_ref).astype(bf16)


def within_kernel(place_ref, xc_ref, xdt_ref, bcc_ref, acum_ref, skip_ref, y_ref):
    width = xc_ref.shape[1]
    first = place_ref[2 * PROMPTS] + pl.program_id(0) * CHUNK
    local = rows_iota(CHUNK)
    token = first + local
    age = token - start_of(token, place_ref)
    behind = local - lax.broadcasted_iota(jnp.int32, (CHUNK, CHUNK), 1)
    bias = jnp.where((behind >= 0) & (behind <= age), 0.0, NEVER)
    scores = lax.dot_general(
        bcc_ref[:, NS:], bcc_ref[:, :NS], (((1,), (1,)), ((), ())), preferred_element_type=f32
    )
    acum = acum_ref[...]
    acum_turned = jnp.transpose(acum)
    low_half = lax.broadcasted_iota(jnp.int32, (CHUNK, LANES), 1) < LANES // 2
    for pair in range(width // LANES):
        columns = slice(pair * LANES, (pair + 1) * LANES)
        mixing = []
        for head in (2 * pair, 2 * pair + 1):
            spread = acum[:, head : head + 1] - acum_turned[head : head + 1] + bias
            mixing.append((jnp.exp(spread) * scores).astype(bf16))
        x_dt = xdt_ref[:, columns].astype(f32)
        stacked = jnp.concatenate(
            [jnp.where(low_half, x_dt, 0.0), jnp.where(low_half, 0.0, x_dt)], axis=0
        ).astype(bf16)
        y_ref[:, columns] = (
            jnp.dot(jnp.concatenate(mixing, axis=1), stacked, preferred_element_type=f32)
            + skip_ref[0:1, columns] * xc_ref[:, columns].astype(f32)
        )


def finish_kernel(
    place_ref, y_ref, bcc_ref, acum_ref, prior_ref, thr_ref, entering_ref, z_ref, gain_ref,
    weight_ref, expand_ref, out_ref, square_ref, scaled,
):
    parts = y_ref.shape[0] // CHUNK
    for part in range(parts):
        rows = slice(part * CHUNK, (part + 1) * CHUNK)
        first = place_ref[2 * PROMPTS] + (pl.program_id(0) * parts + part) * CHUNK
        token = first + rows_iota(CHUNK)
        inflow = jnp.exp(
            jnp.where(start_of(token, place_ref) < first, acum_ref[rows], NEVER)
        )
        state = (
            prior_ref[part].astype(f32)
            + spread_row(thr_ref[part, 0:1], expand_ref) * entering_ref[...]
        ).astype(bf16)
        ssm = y_ref[rows] + spread_heads(inflow, expand_ref) * jnp.dot(
            bcc_ref[rows, NS:], state, preferred_element_type=f32
        )
        z = z_ref[rows].astype(f32)
        gated = ssm * (z * jax.nn.sigmoid(z))
        square_ref[rows] = jnp.sum(gated * gated, axis=1, keepdims=True)
        scaled[rows] = (gated * gain_ref[0:1]).astype(bf16)
    block = out_ref.shape[2]
    for dest in range(out_ref.shape[0]):
        out_ref[dest] = jnp.dot(
            scaled[...],
            weight_ref[:, dest * block : (dest + 1) * block],
            preferred_element_type=f32,
        ).astype(bf16)


def whole(shape):
    return pl.BlockSpec(shape, lambda i: (0,) * len(shape))


def stepped(shape):
    return pl.BlockSpec(shape, lambda i: (i,) + (0,) * (len(shape) - 1))


smem = pl.BlockSpec(memory_space=pltpu.SMEM)


def per_device(
    hidden,
    x_weight,
    z_weight,
    bc_weight,
    dt_weight,
    conv_x,
    conv_bc,
    dt_bias,
    decay_rate,
    skip_gain,
    norm_gain,
    out_weight,
    lengths,
    owners,
):
    rows_here = hidden.shape[0]
    width = x_weight.shape[1]
    heads = dt_bias.shape[0]
    head_width = width // heads
    tp = lax.axis_size("tp")
    seq = lax.axis_size("seq")
    model = out_weight.shape[1]
    my_index = lax.axis_index("seq")
    first_row = my_index * rows_here
    prompt_end = jnp.cumsum(lengths).astype(jnp.int32)
    prompt_start = prompt_end - lengths
    place = jnp.concatenate(
        [prompt_end, prompt_start, jnp.full((8,), first_row, jnp.int32)]
    ).astype(jnp.int32)
    pad = ((0, 0), (0, LANES - heads))
    bias = jnp.broadcast_to(jnp.pad(dt_bias[None], pad), (8, LANES))
    rate = jnp.broadcast_to(jnp.pad(decay_rate[None], pad), (8, LANES))
    skip = jnp.repeat(skip_gain, head_width)[None]
    head_of = jnp.arange(width, dtype=jnp.int32) // head_width
    expand = (
        jnp.arange(2 * LANES, dtype=jnp.int32)[:, None] % LANES == head_of[None, :]
    ).astype(bf16)
    dt_wide = jnp.pad(dt_weight, pad)

    bc_full = lax.all_gather(bc_weight, "tp", axis=1, tiled=True)
    piece = lax.all_gather(hidden, "tp", axis=1, tiled=True)

    def take(rows, matrix):
        return jnp.dot(rows, matrix, preferred_element_type=f32)

    x_in = take(piece, x_weight).astype(bf16)
    bc_in = take(piece, bc_full).astype(bf16)
    tail = jnp.concatenate([x_in[rows_here - HALO :], bc_in[rows_here - HALO :]], axis=1)
    halo = lax.ppermute(tail, "seq", [(i, i + 1) for i in range(seq - 1)])
    later, unused = lax.optimization_barrier((piece, tail))
    z_in = take(later, z_weight).astype(bf16)
    dt_raw = take(later, dt_wide)

    chunks = rows_here // CHUNK
    params = pltpu.CompilerParams(
        dimension_semantics=("arbitrary",), vmem_limit_bytes=40 * 1024 * 1024
    )
    x_conv, x_dt, bc_conv, acum, prior, thr, end, finals = pl.pallas_call(
        states_kernel,
        grid=(chunks,),
        in_specs=[
            smem,
            stepped((CHUNK, width)),
            stepped((CHUNK, 2 * NS)),
            whole((HALO, width)),
            whole((HALO, 2 * NS)),
            stepped((CHUNK, LANES)),
            whole((KCONV, width)),
            whole((KCONV, 2 * NS)),
            whole((8, LANES)),
            whole((8, LANES)),
            whole((2 * LANES, width)),
        ],
        out_specs=[
            stepped((CHUNK, width)),
            stepped((CHUNK, width)),
            stepped((CHUNK, 2 * NS)),
            stepped((CHUNK, LANES)),
            stepped((1, NS, width)),
            stepped((1, 8, LANES)),
            whole((NS + EXTRA, width)),
            whole((PROMPTS, NS + EXTRA, width)),
        ],
        out_shape=[
            jax.ShapeDtypeStruct((rows_here, width), bf16),
            jax.ShapeDtypeStruct((rows_here, width), bf16),
            jax.ShapeDtypeStruct((rows_here, 2 * NS), bf16),
            jax.ShapeDtypeStruct((rows_here, LANES), f32),
            jax.ShapeDtypeStruct((chunks, NS, width), bf16),
            jax.ShapeDtypeStruct((chunks, 8, LANES), f32),
            jax.ShapeDtypeStruct((NS + EXTRA, width), bf16),
            jax.ShapeDtypeStruct((PROMPTS, NS + EXTRA, width), bf16),
        ],
        scratch_shapes=[
            pltpu.VMEM((HALO + CHUNK, width), f32),
            pltpu.VMEM((HALO + CHUNK, 2 * NS), f32),
            pltpu.VMEM((NS, width), f32),
            pltpu.VMEM((8, LANES), f32),
        ],
        compiler_params=params,
        cost_estimate=pl.CostEstimate(
            flops=8 * 10**9, bytes_accessed=16 * 10**6, transcendentals=2 * 10**6
        ),
    )(
        place, x_in, bc_in, halo[:, :width], halo[:, width:], dt_raw, conv_x, conv_bc,
        bias, rate, expand,
    )
    pieces = lax.all_gather(end, "seq")

    y = pl.pallas_call(
        within_kernel,
        grid=(chunks,),
        in_specs=[
            smem,
            stepped((CHUNK, width)),
            stepped((CHUNK, width)),
            stepped((CHUNK, 2 * NS)),
            stepped((CHUNK, LANES)),
            whole((1, width)),
        ],
        out_specs=stepped((CHUNK, width)),
        out_shape=jax.ShapeDtypeStruct((rows_here, width), f32),
        compiler_params=params,
        cost_estimate=pl.CostEstimate(
            flops=8 * 10**9, bytes_accessed=16 * 10**6, transcendentals=2 * 10**6
        ),
    )(place, x_conv, x_dt, bc_conv, acum, skip)

    def heads_of(rows, at):
        return (rows[at].astype(f32) + rows[at + 1].astype(f32))[None]

    keeper = owners[0]
    holder = (prompt_end[keeper] - 1) // rows_here
    entering = jnp.zeros((NS, width), f32)
    entering_kept = entering
    for position in range(seq - 1):
        through = heads_of(pieces[position], NS)
        local_end = pieces[position, :NS].astype(f32)
        entering = jnp.where(position < my_index, through * entering + local_end, entering)
        entering_kept = jnp.where(
            position < holder, through * entering_kept + local_end, entering_kept
        )

    wide = 2 * CHUNK
    partial, square = pl.pallas_call(
        finish_kernel,
        grid=(rows_here // wide,),
        in_specs=[
            smem,
            stepped((wide, width)),
            stepped((wide, 2 * NS)),
            stepped((wide, LANES)),
            stepped((wide // CHUNK, NS, width)),
            stepped((wide // CHUNK, 8, LANES)),
            whole((NS, width)),
            stepped((wide, width)),
            whole((1, width)),
            whole((width, model)),
            whole((2 * LANES, width)),
        ],
        out_specs=[
            pl.BlockSpec((tp, wide, model // tp), lambda i: (0, i, 0)),
            stepped((wide, 1)),
        ],
        out_shape=[
            jax.ShapeDtypeStruct((tp, rows_here, model // tp), bf16),
            jax.ShapeDtypeStruct((rows_here, 1), f32),
        ],
        scratch_shapes=[pltpu.VMEM((wide, width), bf16)],
        compiler_params=params,
        cost_estimate=pl.CostEstimate(
            flops=8 * 10**9, bytes_accessed=16 * 10**6, transcendentals=2 * 10**6
        ),
    )(
        place, y, bc_conv, acum, prior, thr, entering, z_in, norm_gain[None], out_weight, expand
    )
    summed = lax.psum_scatter(partial, "tp", scatter_dimension=0, tiled=False)
    square_sum = lax.psum(square.reshape(rows_here // LANES, LANES), "tp").reshape(rows_here, 1)
    mixed = (summed.astype(f32) * lax.rsqrt(square_sum / DIN + epsilon)).astype(bf16)

    kept = lax.psum(finals, "seq")[keeper]
    count = KCONV - 1
    final = kept[:NS].astype(f32) + heads_of(kept, NS + 2 * count) * entering_kept
    final_state = final.T.reshape(1, heads, head_width, NS)
    conv_edge_x = kept[NS : NS + count][None]
    conv_edge_bc = kept[NS + count : NS + 2 * count, : 2 * NS][None]
    return (mixed, final_state, conv_edge_x, conv_edge_bc)


def solution(mesh):
    return jax.shard_map(
        per_device,
        mesh=mesh,
        in_specs=(
            P("seq", "tp"),
            P(None, "tp"),
            P(None, "tp"),
            P(None, "tp"),
            P(None, "tp"),
            P(None, "tp"),
            P(),
            P("tp"),
            P("tp"),
            P("tp"),
            P("tp"),
            P("tp", None),
            P(),
            P("seq"),
        ),
        out_specs=(
            P("seq", "tp"),
            P("seq", "tp", None, None),
            P("seq", None, "tp"),
            P("seq", None, None),
        ),
        check_vma=False,
    )
```

time: 561 us -> 289 us (0.52); the launches traced: 550 us -> 289 us
  local copies, waits for them, and re-layouts: 152 us -> 24.7 us
  matrix products: 78.8 us -> 19.2 us
  blocking collectives: 64.1 us -> 6 us
  other arithmetic: 40.6 us -> 11 us
  Pallas kernels: 0 us -> 29.2 us
  waiting for transfers between devices: 189 us -> 178 us
  loops' own time: 5.67 us -> 0 us
    dynamic_update_slice x8 -> x0, local copies, waits for them, and re-layouts: 98 us -> none  [per_device(): local_end, (outputs, priors) = lax.scan(advance_block, init_state, packed)]
    dot_general x23 -> x4, matrix products: 78.8 us -> 19.2 us  [take(): return jnp.dot(rows, matrix, preferred_element_type=f32)]
    psum x1, waiting for transfers between devices: 18 us -> 58.3 us  [per_device(): kept = lax.psum(finals, 'seq')[keeper]]
    reduce_scatter x1, waiting for transfers between devices: 72.1 us -> 32.2 us  [per_device(): summed = lax.psum_scatter(partial, 'tp', scatter_dimension=0, tiled=False)]
    psum x2 -> x1, blocking collectives: 42.5 us -> 6 us  [per_device(): lax.psum(square.reshape(rows_here // LANES, LANES), 'tp')]
    pallas_call x0 -> x3, Pallas kernels: none -> 29.2 us  [the longest x1 12.7 us: per_device(): pl.pallas_call(states_kernel, grid=(chunks,), in_specs=[smem, stepped((CH...]
    all_gather x1 -> x0, blocking collectives: 21.6 us -> none  [prefix(): pieces = jax.tree.map(lambda part: lax.all_gather(part, axis), value)]
    dynamic_slice x20 -> x0, local copies, waits for them, and re-layouts: 15.7 us -> none  [per_device(): local_end, (outputs, priors) = lax.scan(advance_block, init_state, packed)]
  transfers between devices with their start and end apart: 6 -> 6, of which waited for: 6 -> 6; matrix products, arithmetic and copies ran while one was open for 11% -> 9% of each run, Pallas kernels for 0% -> 6%
where the time goes in v1:
time: 289 us
  waiting for transfers between devices  178 us (62%)
  Pallas kernels  29.2 us (10%)
  local copies, waits for them, and re-layouts  24.7 us (9%)
  matrix products  19.2 us (7%)
  between operations  17.4 us (6%)
  other arithmetic  11 us (4%)
  blocking collectives  6 us (2%)
  starting transfers between devices  3.76 us (1%)
    psum x1, waiting for transfers between devices, per_device(): kept = lax.psum(finals, 'seq')[keeper]  58.3 us
    all_gather x1, waiting for transfers between devices, per_device(): piece = lax.all_gather(hidden, 'tp', axis=1, tiled=True)  36.1 us
    reduce_scatter x1, waiting for transfers between devices, per_device(): summed = lax.psum_scatter(partial, 'tp', scatter_dimension=0, tiled=False)  32.2 us
    all_gather x1, waiting for transfers between devices, per_device(): pieces = lax.all_gather(end, 'seq')  32.1 us
    dot_general x4, matrix products, take(): return jnp.dot(rows, matrix, preferred_element_type=f32)  19.2 us
    unnamed x42, local copies, waits for them, and re-layouts  18.3 us
    all_gather x1, waiting for transfers between devices, per_device(): bc_full = lax.all_gather(bc_weight, 'tp', axis=1, tiled=True)  17.3 us
    pallas_call x1, Pallas kernels, per_device(): pl.pallas_call(states_kernel, grid=(chunks,), in_specs=[smem, stepped((CH...  12.7 us
  transfers between devices with their start and end apart: 6, of which 6 were waited for; matrix products, arithmetic and copies ran while one was open for 9% of the time, Pallas kernels for 6%

profile of v1, /device:TPU:0, one launch (start us, length us, event | category | flops | bytes accessed | tf_op | source)
XLA Modules:
  0.0 289.0 jit_solution(4878488607295239433)
XLA Ops:
  11.8 17.3 %all-gather.7.cloned.1.call-done = bf16[2048,256]{0,1:T(8,128)(2,1)} async-done(((bf16[2048,64]{0,1:T(8,128)(2,1)}), bf16[2048,256]{0,1:T(8,128)(2,1)}) %all-gather.7.cloned.1.call-update) | async-done | bytes 1048592 | tf_op jit(solution)/shard_map/all_gather | solution.py:285
  29.0 36.1 %all-gather.5.cloned.1.call-done = bf16[1024,2048]{1,0:T(8,128)(2,1)} async-done(((bf16[1024,512]{1,0:T(8,128)(2,1)}), bf16[1024,2048]{1,0:T(8,128)(2,1)}) %all-gather.5.cloned.1.call-update) | async-done | bytes 4194320 | tf_op jit(solution)/shard_map/all_gather | solution.py:286
  65.1 3.9 %convolution_convert_fusion.2.bc_ref = bf16[1024,256]{1,0:T(8,128)(2,1)S(1)} fusion(bf16[1024,2048]{1,0:T(8,128)(2,1)} %all-gather.5.cloned.1.call-done, bf16[2048,256]{0,1:T(8,128)(2,1)} %all-gather.7.cloned.1.call-done), kind=kOutput, calls=%fused_computation.4 | convolution fusion | flops 1074003968 | bytes 5767168 | tf_op jit(solution)/shard_map/dot_general | solution.py:289
  69.0 1.1 copy-done.19
  70.1 4.7 %convolution_convert_fusion.1.x_ref = bf16[1024,1024]{1,0:T(8,128)(2,1)S(1)} fusion(bf16[1024,2048]{1,0:T(8,128)(2,1)S(1)} %copy-done.19, bf16[2048,1024]{1,0:T(8,128)(2,1)S(1)} %copy-done.18), kind=kOutput, calls=%fused_computation.3 | convolution fusion | flops 4296015872 | bytes 10485760 | tf_op jit(solution)/shard_map/dot_general | solution.py:289
  74.9 3.4 %collective-permute-start = (bf16[16,1280]{1,0:T(8,128)(2,1)S(1)}, bf16[16,1280]{1,0:T(8,128)(2,1)S(1)}, u32[]{:S(2)}, u32[]{:S(2)}) collective-permute-start(bf16[16,1280]{1,0:T(8,128)(2,1)S(1)} %pad_maximum_fusion), channel_id=1, source_target_pairs={{0,4},{4,8},{8,12},{12,16},{16,20},{20,24},{24,28},{1,5},{5,9},{9,... | collective-permute-start | bytes 122888 | tf_op jit(solution)/shard_map/ppermute | solution.py:294
  78.3 1.2 fusion.20.dt_ref
  80.0 12.7 %shard_map.165 = (bf16[1024,1024]{1,0:T(8,128)(2,1)S(1)}, bf16[1024,1024]{1,0:T(8,128)(2,1)S(1)}, bf16[1024,256]{1,0:T(8,128)(2,1)S(1)}, f32[1024,128]{1,0:T(8,1...) custom-call(s32[16]{0:T(128)S(1)} %pad_add_fusion.place_ref, ...), custom_call_target="tpu_custom_call" | custom-call | flops 8000000000 | bytes 16000000 | tf_op jit(solution)/shard_map/pallas_call | solution.py:303
  92.7 1.4 copy-done.6
  94.0 1.4 copy-done.8
  97.2 9.4 %convolution_convert_fusion.z_ref = bf16[1024,1024]{1,0:T(8,128)(2,1)} fusion(bf16[1024,2048]{1,0:T(8,128)(2,1)} %all-gather.5.cloned.1.call-done, bf16[2048,1024]{1,0:T(8,128)(2,1)} %param.16), kind=kOutput, calls=%fused_computation.2 | convolution fusion | flops 4296015872 | bytes 10485760 | tf_op jit(solution)/shard_map/dot_general | solution.py:289
  106.9 1.6 copy-done.7
  108.5 1.6 copy-done.9
  110.1 1.0 copy-done.11
  111.2 1.0 copy-done.14
  112.2 5.4 %shard_map.166.y_ref = f32[1024,1024]{1,0:T(8,128)S(1)} custom-call(s32[16]{0:T(128)S(1)} %pad_add_fusion.place_ref, bf16[1024,1024]{1,0:T(8,128)(2,1)S(1)} %copy-done.7, bf16[1024,1024]{1,0:T(8,128)(2,1)S(1)} %copy-done.9, bf16[1024,256]{1,0:T(8,128)(2,1)S(1)} %copy-done.11, f32[1024,128]{1,0:T(8,128)S(1)} %copy-done.14, ...), custom_call_target="tpu_custom_call" | custom-call | flops 8000000000 | bytes 16000000 | tf_op jit(solution)/shard_map/pallas_call | solution.py:355
  117.6 1.9 copy-done.4
  119.5 32.1 %all-gather.9.cloned.1.call-done = bf16[1152,1024]{1,0:T(8,128)(2,1)} async-done(((bf16[144,1024]{1,0:T(8,128)(2,1)}), bf16[1152,1024]{1,0:T(8,128)(2,1)}) %all-gather.9.cloned.1.call-update) | async-done | bytes 2359312 | tf_op jit(solution)/shard_map/all_gather | solution.py:353
  151.6 1.0 fusion.32
  152.6 1.9 fusion.11.entering_ref
  154.5 1.6 copy-done.5
  156.1 1.0 copy-done.12
  157.1 1.0 copy-done.15
  158.2 11.1 %shard_map.167 = (bf16[4,1024,512]{2,1,0:T(8,128)(2,1)S(1)}, f32[1024,1]{1,0:T(8,128)S(1)}) custom-call(s32[16]{0:T(128)S(1)} %pad_add_fusion.place_ref, f32[1024,1024]{1,0:T(8,128)} %copy-done.4, bf16[1024,256]{1,0:T(8,128)(2,1)S(1)} %copy-done.12, f32[1024,128]{1,0:T(8,128)S(1)} %copy-done.15, bf16[8,128,1024]{2,1,0:T(8,128)(2,1)S(1)} %get-tuple-element.20.prior_ref, ...), custom_call_target="tpu_custom_call" | custom-call | flops 8000000000 | bytes 16000000 | tf_op jit(solution)/shard_map/pallas_call | solution.py:390
  169.3 1.9 copy-done
  175.3 58.3 %all-reduce.5.cloned.1.call-done = bf16[4,144,1024]{2,1,0:T(8,128)(2,1)} async-done(((bf16[4,144,1024]{2,1,0:T(8,128)(2,1)}), bf16[4,144,1024]{2,1,0:T(8,128)(2,1)}) %all-reduce.5.cloned.1.call-update) | async-done | bytes 1179664 | tf_op jit(solution)/shard_map/psum | solution.py:426
  234.4 1.3 constant_dynamic-slice_fusion
  237.3 2.3 fusion.15
  239.5 2.0 copy.19
  241.8 6.0 %psum.14 = f32[8,128]{1,0:T(8,128)S(1)} all-reduce(f32[8,128]{1,0:T(8,128)S(1)} %bitcast.118), channel_id=1, replica_groups=mesh['seq'=8,'tp'=4] {'tp'}, use_global_device_ids=true, to_apply=%region_2.3 | all-reduce | flops 1024 | bytes 8192 | tf_op jit(solution)/shard_map/psum | solution.py:423
  247.8 32.2 %reduce-scatter.2.cloned.1.call-done = bf16[1,1024,512]{2,1,0:T(8,128)(2,1)} async-done(((bf16[4,1024,512]{2,1,0:T(8,128)(2,1)}), bf16[1,1024,512]{2,1,0:T(8,128)(2,1)}) %reduce-scatter.2.cloned.1.call-update) | async-done | bytes 1048592 | tf_op jit(solution)/shard_map/reduce_scatter | solution.py:422
  280.0 2.5 fusion
  (65 shorter events, 10.2 us)
Async XLA Ops:
  7.2 21.8 %all-gather.7.cloned.1.call-start = ((), (), s32[]{:S(2)}) async-start(), calls=%async_computation.2 | async-start | bytes 1310720 | tf_op jit(solution)/shard_map/all_gather | solution.py:285
  7.9 57.2 %all-gather.5.cloned.1.call-start = ((), (), s32[]{:S(2)}) async-start(), calls=%async_computation.1 | async-start | bytes 5242880 | tf_op jit(solution)/shard_map/all_gather | solution.py:286
  8.6 143.0 %all-gather.9.cloned.1.call-start = ((), (), s32[]{:S(2)}) async-start(), calls=%async_computation.5 | async-start | bytes 2654208 | tf_op jit(solution)/shard_map/all_gather | solution.py:353
  65.1 4.0 %copy-start.18 = (bf16[2048,1024]{1,0:T(8,128)(2,1)S(1)}, bf16[2048,1024]{1,0:T(8,128)(2,1)}, u32[]{:S(2)}) copy-start(bf16[2048,1024]{1,0:T(8,128)(2,1)} %param.15) | copy-start | bytes 12582916
  65.1 5.0 %copy-start.19 = (bf16[1024,2048]{1,0:T(8,128)(2,1)S(1)}, bf16[1024,2048]{1,0:T(8,128)(2,1)}, u32[]{:S(2)}) copy-start(bf16[1024,2048]{1,0:T(8,128)(2,1)} %all-gather.5.cloned.1.call-done) | copy-start | bytes 12582916
  70.1 8.1 %copy-start.20 = (bf16[2048,16]{0,1:T(8,128)(2,1)S(1)}, bf16[2048,16]{0,1:T(8,128)(2,1)}, u32[]{:S(2)}) copy-start(bf16[2048,16]{0,1:T(8,128)(2,1)} %param.18) | copy-start | bytes 196612
  74.8 5.1 %copy-start.1 = (f32[4,1024]{1,0:T(4,128)S(1)}, f32[4,1024]{1,0:T(4,128)}, u32[]{:S(2)}) copy-start(f32[4,1024]{1,0:T(4,128)} %taps_x_ref.1) | copy-start | bytes 49156
  74.8 5.1 %copy-start.2 = (f32[4,256]{1,0:T(4,128)S(1)}, f32[4,256]{1,0:T(4,128)}, u32[]{:S(2)}) copy-start(f32[4,256]{1,0:T(4,128)} %taps_bc_ref.1) | copy-start | bytes 12292
  74.9 5.0 %collective-permute-start = (bf16[16,1280]{1,0:T(8,128)(2,1)S(1)}, bf16[16,1280]{1,0:T(8,128)(2,1)S(1)}, u32[]{:S(2)}, u32[]{:S(2)}) collective-permute-start(bf16[16,1280]{1,0:T(8,128)(2,1)S(1)} %pad_maximum_fusion), channel_id=1, source_target_pairs={{0,4},{4,8},{8,12},{12,16},{16,20},{20,24},{24,28},{1,5},{5,9},{9,... | collective-permute-start | bytes 122888 | tf_op jit(solution)/shard_map/ppermute | solution.py:294
  79.9 17.1 %copy-start.17 = (f32[16]{0:T(128)S(1)}, f32[16]{0:T(128)}, u32[]{:S(2)}) copy-start(f32[16]{0:T(128)} %param.23) | copy-start | bytes 196
  92.7 1.4 copy-start.6
  94.0 1.4 copy-start.8
  95.4 0.8 copy-start.10
  96.2 0.8 copy-start.13
  97.0 136.5 %all-reduce.5.cloned.1.call-start = ((), (), s32[]{:S(2)}) async-start(), calls=%async_computation.4 | async-start | bytes 2359296 | tf_op jit(solution)/shard_map/psum | solution.py:426
  106.6 173.3 %reduce-scatter.2.cloned.1.call-start = ((), (), s32[]{:S(2)}) async-start(), calls=%async_computation.3 | async-start | bytes 5242880 | tf_op jit(solution)/shard_map/reduce_scatter | solution.py:422
  106.9 1.6 copy-start.7
  108.5 1.6 copy-start.9
  110.1 1.0 copy-start.11
  111.2 1.0 copy-start.14
  112.2 42.3 %copy-start.3 = (f32[1024]{0:T(1024)S(1)}, f32[1024]{0:T(1024)}, u32[]{:S(2)}) copy-start(f32[1024]{0:T(1024)} %param.24) | copy-start | bytes 12292
  117.6 1.9 copy-start.4
  154.5 1.6 copy-start.5
  156.1 1.0 copy-start.12
  157.1 1.0 copy-start.15
  169.3 1.9 copy-start
  171.2 66.0 %copy-start.16 = (bf16[1152,1024]{1,0:T(8,128)(2,1)S(1)}, bf16[1152,1024]{1,0:T(8,128)(2,1)}, u32[]{:S(2)}) copy-start(bf16[1152,1024]{1,0:T(8,128)(2,1)} %all-gather.9.cloned.1.call-done) | copy-start | bytes 7077892
Sparse Core Ops, SparseCore 0:
  9.6 19.4 all-gather.6
  30.6 34.4 all-gather.4
  97.1 54.4 all-gather.8
  155.0 78.5 all-reduce.4
  236.1 43.8 reduce-scatter.1

commit v2 on v1

--- a/solution.py
+++ b/solution.py
@@ -166,7 +166,11 @@
     @pl.when(step == pl.num_programs(0) - 1)
     def _():
         end_ref[0:NS] = state[...].astype(bf16)
-        end_ref[NS : NS + EXTRA] = split_rows(through[0:1], 0, expand_ref).astype(bf16)
+        owner = place_ref[2 * PROMPTS + 1].astype(f32)
+        end_ref[NS : NS + EXTRA] = (
+            split_rows(through[0:1], 0, expand_ref)
+            + jnp.where(rows_iota(EXTRA, width) == 2, owner, 0.0)
+        ).astype(bf16)
 
 
 def within_kernel(place_ref, xc_ref, xdt_ref, bcc_ref, acum_ref, skip_ref, y_ref):
@@ -270,7 +274,12 @@
     prompt_end = jnp.cumsum(lengths).astype(jnp.int32)
     prompt_start = prompt_end - lengths
     place = jnp.concatenate(
-        [prompt_end, prompt_start, jnp.full((8,), first_row, jnp.int32)]
+        [
+            prompt_end,
+            prompt_start,
+            jnp.full((1,), first_row, jnp.int32),
+            jnp.broadcast_to(owners, (7,)),
+        ]
     ).astype(jnp.int32)
     pad = ((0, 0), (0, LANES - heads))
     bias = jnp.broadcast_to(jnp.pad(dt_bias[None], pad), (8, LANES))
@@ -423,7 +432,29 @@
     square_sum = lax.psum(square.reshape(rows_here // LANES, LANES), "tp").reshape(rows_here, 1)
     mixed = (summed.astype(f32) * lax.rsqrt(square_sum / DIN + epsilon)).astype(bf16)
 
-    kept = lax.psum(finals, "seq")[keeper]
+    wanted = pieces[:, NS + 2, 0].astype(jnp.int32)
+
+    def slots_for(prompts):
+        chosen = prompts[:, None, None]
+        total = jnp.where(chosen == 0, finals[0][None], jnp.zeros((), bf16))
+        for r in range(1, PROMPTS):
+            total = jnp.where(chosen == r, finals[r][None], total)
+        return total
+
+    slots = None
+    for bit in range(seq.bit_length() - 1):
+        mine = (my_index >> bit) & 1
+        if bit == 0:
+            pairs = wanted.reshape(seq // 2, 2)
+            own = slots_for(jnp.where(mine == 0, pairs[:, 0], pairs[:, 1]))
+            sent = slots_for(jnp.where(mine == 0, pairs[:, 1], pairs[:, 0]))
+        else:
+            pairs = slots.reshape((slots.shape[0] // 2, 2) + slots.shape[1:])
+            own = jnp.where(mine == 0, pairs[:, 0], pairs[:, 1])
+            sent = jnp.where(mine == 0, pairs[:, 1], pairs[:, 0])
+        partners = [(i, i ^ (1 << bit)) for i in range(seq)]
+        slots = own + lax.ppermute(sent, "seq", partners)
+    kept = slots[0]
     count = KCONV - 1
     final = kept[:NS].astype(f32) + heads_of(kept, NS + 2 * count) * entering_kept
     final_state = final.T.reshape(1, heads, head_width, NS)

time: 289 us -> 236 us (0.82)
  waiting for transfers between devices: 178 us -> 121 us
  local copies, waits for them, and re-layouts: 24.7 us -> 16.5 us
  starting transfers between devices: 3.76 us -> 9.03 us
  other arithmetic: 11 us -> 14.8 us
  matrix products: 19.2 us -> 22.6 us
    psum x1 -> x0, waiting for transfers between devices: 58.3 us -> none  [per_device(): kept = lax.psum(finals, 'seq')[keeper]]
    ppermute x0 -> x3, waiting for transfers between devices: none -> 39.3 us  [per_device(): slots = own + lax.ppermute(sent, 'seq', partners)]
    reduce_scatter x1, waiting for transfers between devices: 32.2 us -> 0.01 us  [per_device(): summed = lax.psum_scatter(partial, 'tp', scatter_dimension=0, tiled=False)]
    all_gather x1, waiting for transfers between devices: 17.3 us -> 9.02 us  [per_device(): bc_full = lax.all_gather(bc_weight, 'tp', axis=1, tiled=True)]
    unnamed x42 -> x40, local copies, waits for them, and re-layouts: 18.3 us -> 11.9 us
    ppermute x0 -> x3, starting transfers between devices: none -> 5.19 us  [per_device(): slots = own + lax.ppermute(sent, 'seq', partners)]
    all_gather x1, waiting for transfers between devices: 32.1 us -> 36.9 us  [per_device(): pieces = lax.all_gather(end, 'seq')]
    dot_general x4, matrix products: 19.2 us -> 22.6 us  [take(): return jnp.dot(rows, matrix, preferred_element_type=f32)]
  transfers between devices with their start and end apart: 6 -> 8, of which waited for: 6 -> 7; matrix products, arithmetic and copies ran while one was open for 9% -> 14% of each run, Pallas kernels for 6% -> 2%
where the time goes in v2:
time: 236 us
  waiting for transfers between devices  121 us (51%)
  Pallas kernels  28.5 us (12%)
  matrix products  22.6 us (10%)
  between operations  17.3 us (7%)
  local copies, waits for them, and re-layouts  16.5 us (7%)
  other arithmetic  14.8 us (6%)
  starting transfers between devices  9.03 us (4%)
  blocking collectives  6.07 us (3%)
    ppermute x3, waiting for transfers between devices, per_device(): slots = own + lax.ppermute(sent, 'seq', partners)  39.3 us
    all_gather x1, waiting for transfers between devices, per_device(): pieces = lax.all_gather(end, 'seq')  36.9 us
    all_gather x1, waiting for transfers between devices, per_device(): piece = lax.all_gather(hidden, 'tp', axis=1, tiled=True)  34.4 us
    dot_general x4, matrix products, take(): return jnp.dot(rows, matrix, preferred_element_type=f32)  22.6 us
    pallas_call x1, Pallas kernels, per_device(): pl.pallas_call(states_kernel, grid=(chunks,), in_specs=[smem, stepped((CH...  12.3 us
    unnamed x40, local copies, waits for them, and re-layouts  11.9 us
    pallas_call x1, Pallas kernels, per_device(): pl.pallas_call(finish_kernel, grid=(rows_here // wide,), in_specs=[smem,...  10.9 us
    all_gather x1, waiting for transfers between devices, per_device(): bc_full = lax.all_gather(bc_weight, 'tp', axis=1, tiled=True)  9.02 us
  transfers between devices with their start and end apart: 8, of which 7 were waited for; matrix products, arithmetic and copies ran while one was open for 14% of the time, Pallas kernels for 2%

profile of v2, /device:TPU:0, one launch (start us, length us, event | category | flops | bytes accessed | tf_op | source)
XLA Modules:
  0.0 236.2 jit_solution(13608543563897093549)
XLA Ops:
  12.4 34.4 %all-gather.5.cloned.1.call-done = bf16[1024,2048]{1,0:T(8,128)(2,1)} async-done(((bf16[1024,512]{1,0:T(8,128)(2,1)}), bf16[1024,2048]{1,0:T(8,128)(2,1)}) %all-gather.5.cloned.1.call-update) | async-done | bytes 4194320 | tf_op jit(solution)/shard_map/all_gather | solution.py:295
  46.8 7.9 %convolution_convert_fusion.1.x_ref = bf16[1024,1024]{1,0:T(8,128)(2,1)S(1)} fusion(bf16[1024,2048]{1,0:T(8,128)(2,1)} %all-gather.5.cloned.1.call-done, bf16[2048,1024]{1,0:T(8,128)(2,1)} %param.15), kind=kOutput, calls=%fused_computation.3 | convolution fusion | flops 4296015872 | bytes 10485760 | tf_op jit(solution)/shard_map/dot_general | solution.py:298
  54.8 1.3 copy-done.1
  56.1 9.0 %all-gather.7.cloned.1.call-done = bf16[2048,256]{0,1:T(8,128)(2,1)} async-done(((bf16[2048,64]{0,1:T(8,128)(2,1)}), bf16[2048,256]{0,1:T(8,128)(2,1)}) %all-gather.7.cloned.1.call-update) | async-done | bytes 1048592 | tf_op jit(solution)/shard_map/all_gather | solution.py:294
  65.1 3.9 %convolution_convert_fusion.2.bc_ref = bf16[1024,256]{1,0:T(8,128)(2,1)S(1)} fusion(bf16[1024,2048]{1,0:T(8,128)(2,1)} %all-gather.5.cloned.1.call-done, bf16[2048,256]{0,1:T(8,128)(2,1)} %all-gather.7.cloned.1.call-done), kind=kOutput, calls=%fused_computation.4 | convolution fusion | flops 1074003968 | bytes 5767168 | tf_op jit(solution)/shard_map/dot_general | solution.py:298
  69.1 3.5 %collective-permute-start = (bf16[16,1280]{1,0:T(8,128)(2,1)S(1)}, bf16[16,1280]{1,0:T(8,128)(2,1)S(1)}, u32[]{:S(2)}, u32[]{:S(2)}) collective-permute-start(bf16[16,1280]{1,0:T(8,128)(2,1)S(1)} %pad_maximum_fusion), channel_id=1, source_target_pairs={{0,4},{4,8},{8,12},{12,16},{16,20},{20,24},{24,28},{1,5},{5,9},{9,... | collective-permute-start | bytes 122888 | tf_op jit(solution)/shard_map/ppermute | solution.py:303
  72.6 1.2 fusion.21.dt_ref
  74.3 12.3 %shard_map.165 = (bf16[1024,1024]{1,0:T(8,128)(2,1)S(1)}, bf16[1024,1024]{1,0:T(8,128)(2,1)S(1)}, bf16[1024,256]{1,0:T(8,128)(2,1)S(1)}, f32[1024,128]{1,0:T(8,1...) custom-call(s32[16]{0:T(128)S(1)} %pad_add_fusion.place_ref, ...), custom_call_target="tpu_custom_call" | custom-call | flops 8000000000 | bytes 16000000 | tf_op jit(solution)/shard_map/pallas_call | solution.py:312
  86.6 1.4 copy-done.7
  88.0 1.3 copy-done.10
  89.3 1.3 copy-done.12
  91.1 9.5 %convolution_convert_fusion.z_ref = bf16[1024,1024]{1,0:T(8,128)(2,1)} fusion(bf16[1024,2048]{1,0:T(8,128)(2,1)} %all-gather.5.cloned.1.call-done, bf16[2048,1024]{1,0:T(8,128)(2,1)} %param.16), kind=kOutput, calls=%fused_computation.2 | convolution fusion | flops 4296015872 | bytes 10485760 | tf_op jit(solution)/shard_map/dot_general | solution.py:298
  100.6 5.4 %shard_map.166.y_ref = f32[1024,1024]{1,0:T(8,128)S(1)} custom-call(s32[16]{0:T(128)S(1)} %pad_add_fusion.place_ref, bf16[1024,1024]{1,0:T(8,128)(2,1)S(1)} %copy-done.11, bf16[1024,1024]{1,0:T(8,128)(2,1)S(1)} %copy-done.13, bf16[1024,256]{1,0:T(8,128)(2,1)S(1)} %get-tuple-element.18.bcc_ref, f32[1024,128]{1,0:T(8,128)S(1)} %get-tuple-element.19.acum_ref, ...), custom_call_target="tpu_custom_call" | custom-call | flops 8000000000 | bytes 16000000 | tf_op jit(solution)/shard_map/pallas_call | solution.py:364
  105.9 1.9 copy-done.6
  107.9 36.9 %all-gather.9.cloned.1.call-done = bf16[1152,1024]{1,0:T(8,128)(2,1)} async-done(((bf16[144,1024]{1,0:T(8,128)(2,1)}), bf16[1152,1024]{1,0:T(8,128)(2,1)}) %all-gather.9.cloned.1.call-update) | async-done | bytes 2359312 | tf_op jit(solution)/shard_map/all_gather | solution.py:362
  144.8 1.1 fusion.34
  145.8 1.9 fusion.12.entering_ref
  147.8 1.6 copy-done.9
  149.4 10.9 %shard_map.167 = (bf16[4,1024,512]{2,1,0:T(8,128)(2,1)S(1)}, f32[1024,1]{1,0:T(8,128)S(1)}) custom-call(s32[16]{0:T(128)S(1)} %pad_add_fusion.place_ref, f32[1024,1024]{1,0:T(8,128)} %copy-done.6, bf16[1024,256]{1,0:T(8,128)(2,1)S(1)} %get-tuple-element.18.bcc_ref, f32[1024,128]{1,0:T(8,128)S(1)} %get-tuple-element.19.acum_ref, ...), custom_call_target="tpu_custom_call" | custom-call | flops 8000000000 | bytes 16000000 | tf_op jit(solution)/shard_map/pallas_call | solution.py:399
  160.2 1.9 copy-done
  163.6 1.3 select_select_fusion
  165.6 26.0 %collective-permute-done.1 = bf16[4,144,1024]{2,1,0:T(8,128)(2,1)S(1)} collective-permute-done((bf16[4,144,1024]{2,1,0:T(8,128)(2,1)}, bf16[4,144,1024]{2,1,0:T(8,128)(2,1)S(1)}, u32[]{:S(2)}, u32[]{:S(2)}) %collective-permute-start.1) | collective-permute-done | bytes 1179680 | tf_op jit(solution)/shard_map/ppermute | solution.py:456
  191.6 1.0 copy-done.15
  192.7 1.7 select_add_fusion
  194.4 1.7 collective-permute-start.2
  196.1 11.4 %collective-permute-done.2 = bf16[2,144,1024]{2,1,0:T(8,128)(2,1)S(1)} collective-permute-done((bf16[2,144,1024]{2,1,0:T(8,128)(2,1)S(1)}, bf16[2,144,1024]{2,1,0:T(8,128)(2,1)S(1)}, u32[]{:S(2)}, u32[]{:S(2)}) %collective-permute-start.2) | collective-permute-done | bytes 589856 | tf_op jit(solution)/shard_map/ppermute | solution.py:456
  208.4 3.0 %collective-permute-start.3 = (bf16[1,144,1024]{2,1,0:T(8,128)(2,1)}, bf16[1,144,1024]{2,1,0:T(8,128)(2,1)}, u32[]{:S(2)}, u32[]{:S(2)}) collective-permute-start(bf16[1,144,1024]{2,1,0:T(8,128)(2,1)} %select_bitcast_fusion.1), channel_id=1, source_target_pairs={{0,16},{4,20},{8,24},{12,28},{16,0},{20,4},{24,8},{28,12},{1,17},{... | collective-permute-start | bytes 884744 | tf_op jit(solution)/shard_map/ppermute | solution.py:456
  214.8 6.1 %psum.7 = f32[8,128]{1,0:T(8,128)S(1)} all-reduce(f32[8,128]{1,0:T(8,128)S(1)} %bitcast.156), channel_id=1, replica_groups=mesh['seq'=8,'tp'=4] {'tp'}, use_global_device_ids=true, to_apply=%region_2.3 | all-reduce | flops 1024 | bytes 8192 | tf_op jit(solution)/shard_map/psum | solution.py:432
  220.8 1.8 collective-permute-done.3
  222.6 1.0 bitcast_add_fusion.1
  225.9 1.3 slice_bitcast_fusion.14
  227.2 2.5 %fusion = bf16[1024,512]{1,0:T(8,128)(2,1)} fusion(bf16[1,1024,512]{2,1,0:T(8,128)(2,1)} %reduce-scatter.2.cloned.1.call-done, f32[1024]{0:T(1024)S(1)} %rsqrt_bitcast_fusion), kind=kLoop, calls=%fused_computation.1 | loop fusion | flops 1572864 | bytes 2101248 | tf_op jit(solution)/shard_map/convert_element_type | solution.py:433
  (77 shorter events, 11.4 us)
Async XLA Ops:
  7.2 39.6 %all-gather.5.cloned.1.call-start = ((), (), s32[]{:S(2)}) async-start(), calls=%async_computation.1 | async-start | bytes 5242880 | tf_op jit(solution)/shard_map/all_gather | solution.py:295
  7.9 57.2 %all-gather.7.cloned.1.call-start = ((), (), s32[]{:S(2)}) async-start(), calls=%async_computation.2 | async-start | bytes 1310720 | tf_op jit(solution)/shard_map/all_gather | solution.py:294
  8.6 136.1 %all-gather.9.cloned.1.call-start = ((), (), s32[]{:S(2)}) async-start(), calls=%async_computation.4 | async-start | bytes 2654208 | tf_op jit(solution)/shard_map/all_gather | solution.py:362
  54.7 1.3 copy-start.1
  56.1 16.5 %copy-start.19 = (bf16[2048,16]{0,1:T(8,128)(2,1)S(1)}, bf16[2048,16]{0,1:T(8,128)(2,1)}, u32[]{:S(2)}) copy-start(bf16[2048,16]{0,1:T(8,128)(2,1)} %param.18) | copy-start | bytes 196612
  65.1 7.5 %copy-start.18 = (bf16[1024,2048]{1,0:T(8,128)(2,1)S(1)}, bf16[1024,2048]{1,0:T(8,128)(2,1)}, u32[]{:S(2)}) copy-start(bf16[1024,2048]{1,0:T(8,128)(2,1)} %all-gather.5.cloned.1.call-done) | copy-start | bytes 12582916
  69.0 5.2 %copy-start.2 = (bf16[1024,1024]{1,0:T(8,128)(2,1)S(1)}, bf16[1024,1024]{1,0:T(8,128)(2,1)}, u32[]{:S(2)}) copy-start(bf16[1024,1024]{1,0:T(8,128)(2,1)} %copy-done.1) | copy-start | bytes 6291460
  69.1 5.2 %copy-start.3 = (f32[4,1024]{1,0:T(4,128)S(1)}, f32[4,1024]{1,0:T(4,128)}, u32[]{:S(2)}) copy-start(f32[4,1024]{1,0:T(4,128)} %taps_x_ref.1) | copy-start | bytes 49156
  69.1 5.2 %copy-start.4 = (f32[4,256]{1,0:T(4,128)S(1)}, f32[4,256]{1,0:T(4,128)}, u32[]{:S(2)}) copy-start(f32[4,256]{1,0:T(4,128)} %taps_bc_ref.1) | copy-start | bytes 12292
  69.1 5.2 %collective-permute-start = (bf16[16,1280]{1,0:T(8,128)(2,1)S(1)}, bf16[16,1280]{1,0:T(8,128)(2,1)S(1)}, u32[]{:S(2)}, u32[]{:S(2)}) collective-permute-start(bf16[16,1280]{1,0:T(8,128)(2,1)S(1)} %pad_maximum_fusion), channel_id=1, source_target_pairs={{0,4},{4,8},{8,12},{12,16},{16,20},{20,24},{24,28},{1,5},{5,9},{9,... | collective-permute-start | bytes 122888 | tf_op jit(solution)/shard_map/ppermute | solution.py:303
  74.3 16.6 %copy-start.17 = (f32[16]{0:T(128)S(1)}, f32[16]{0:T(128)}, u32[]{:S(2)}) copy-start(f32[16]{0:T(128)} %param.23) | copy-start | bytes 196
  86.6 1.4 copy-start.7
  88.0 1.3 copy-start.10
  89.3 1.3 copy-start.12
  90.7 136.5 %reduce-scatter.2.cloned.1.call-start = ((), (), s32[]{:S(2)}) async-start(), calls=%async_computation.3 | async-start | bytes 5242880 | tf_op jit(solution)/shard_map/reduce_scatter | solution.py:431
  91.1 9.5 %copy-start.11 = (bf16[1024,1024]{1,0:T(8,128)(2,1)S(1)}, bf16[1024,1024]{1,0:T(8,128)(2,1)}, u32[]{:S(2)}) copy-start(bf16[1024,1024]{1,0:T(8,128)(2,1)} %copy-done.10) | copy-start | bytes 6291460
  91.1 9.5 %copy-start.13 = (bf16[1024,1024]{1,0:T(8,128)(2,1)S(1)}, bf16[1024,1024]{1,0:T(8,128)(2,1)}, u32[]{:S(2)}) copy-start(bf16[1024,1024]{1,0:T(8,128)(2,1)} %copy-done.12) | copy-start | bytes 6291460
  105.9 1.9 copy-start.6
  107.9 39.9 %copy-start.5 = (f32[1024]{0:T(1024)S(1)}, f32[1024]{0:T(1024)}, u32[]{:S(2)}) copy-start(f32[1024]{0:T(1024)} %param.24) | copy-start | bytes 12292
  144.8 3.0 %copy-start.8 = (bf16[8,128,1024]{2,1,0:T(8,128)(2,1)S(1)}, bf16[8,128,1024]{2,1,0:T(8,128)(2,1)}, u32[]{:S(2)}) copy-start(bf16[8,128,1024]{2,1,0:T(8,128)(2,1)} %copy-done.7) | copy-start | bytes 6291460
  147.8 1.6 copy-start.9
  160.2 1.9 copy-start
  164.9 26.7 %collective-permute-start.1 = (bf16[4,144,1024]{2,1,0:T(8,128)(2,1)}, bf16[4,144,1024]{2,1,0:T(8,128)(2,1)S(1)}, u32[]{:S(2)}, u32[]{:S(2)}) collective-permute-start(bf16[4,144,1024]{2,1,0:T(8,128)(2,1)} %select_select_fusion), channel_id=1, source_target_pairs={{0,4},{4,0},{8,12},{12,8},{16,20},{20,16},{24,28},{28,24},{1,5},{5... | collective-permute-start | bytes 3538952 | tf_op jit(solution)/shard_map/ppermute | solution.py:456
  191.6 1.0 copy-start.15
  194.4 13.1 %collective-permute-start.2 = (bf16[2,144,1024]{2,1,0:T(8,128)(2,1)S(1)}, bf16[2,144,1024]{2,1,0:T(8,128)(2,1)S(1)}, u32[]{:S(2)}, u32[]{:S(2)}) collective-permute-start(bf16[2,144,1024]{2,1,0:T(8,128)(2,1)S(1)} %select_bitcast_fusion), channel_id=1, source_target_pairs={{0,8},{4,12},{8,0},{12,4},{16,24},{20,28},{24,16},{28,20},{1,9},{5... | collective-permute-start | bytes 1769480 | tf_op jit(solution)/shard_map/ppermute | solution.py:456
  207.6 16.7 %copy-start.14 = (bf16[1152,1024]{1,0:T(8,128)(2,1)S(1)}, bf16[1152,1024]{1,0:T(8,128)(2,1)}, u32[]{:S(2)}) copy-start(bf16[1152,1024]{1,0:T(8,128)(2,1)} %all-gather.9.cloned.1.call-done) | copy-start | bytes 7077892
  208.4 14.3 %collective-permute-start.3 = (bf16[1,144,1024]{2,1,0:T(8,128)(2,1)}, bf16[1,144,1024]{2,1,0:T(8,128)(2,1)}, u32[]{:S(2)}, u32[]{:S(2)}) collective-permute-start(bf16[1,144,1024]{2,1,0:T(8,128)(2,1)} %select_bitcast_fusion.1), channel_id=1, source_target_pairs={{0,16},{4,20},{8,24},{12,28},{16,0},{20,4},{24,8},{28,12},{1,17},{... | collective-permute-start | bytes 884744 | tf_op jit(solution)/shard_map/ppermute | solution.py:456
  223.6 0.7 copy-start.16
Sparse Core Ops, SparseCore 0:
  9.6 37.1 all-gather.4
  48.3 16.7 all-gather.6
  90.8 53.9 all-gather.8
  162.3 43.0 reduce-scatter.1

commit v3 on v2

--- a/solution.py
+++ b/solution.py
@@ -292,7 +292,19 @@
     dt_wide = jnp.pad(dt_weight, pad)
 
     bc_full = lax.all_gather(bc_weight, "tp", axis=1, tiled=True)
-    piece = lax.all_gather(hidden, "tp", axis=1, tiled=True)
+    mine_tp = lax.axis_index("tp")
+    blocks = [hidden]
+    apart = [0]
+    bit = tp // 2
+    while bit:
+        partners = [(i, i ^ bit) for i in range(tp)]
+        blocks = blocks + [lax.ppermute(block, "tp", partners) for block in blocks]
+        apart = apart + [distance ^ bit for distance in apart]
+        bit //= 2
+    share = hidden.shape[1]
+    piece = jnp.zeros((rows_here, tp * share), bf16)
+    for block, distance in zip(blocks, apart):
+        piece = lax.dynamic_update_slice_in_dim(piece, block, (mine_tp ^ distance) * share, 1)
 
     def take(rows, matrix):
         return jnp.dot(rows, matrix, preferred_element_type=f32)

time: 236 us -> 223 us (0.945)
  waiting for transfers between devices: 121 us -> 105 us
  starting transfers between devices: 9.03 us -> 12.4 us
  matrix products: 22.6 us -> 19.3 us
  local copies, waits for them, and re-layouts: 16.5 us -> 19.8 us
    all_gather x1 -> x0, waiting for transfers between devices: 34.4 us -> none  [per_device(): piece = lax.all_gather(hidden, 'tp', axis=1, tiled=True)]
    ppermute x0 -> x3, waiting for transfers between devices: none -> 26.8 us  [per_device(): blocks = blocks + [lax.ppermute(block, 'tp', partners) for block in blocks]]
    all_gather x1, waiting for transfers between devices: 9.02 us -> 0.01 us  [per_device(): bc_full = lax.all_gather(bc_weight, 'tp', axis=1, tiled=True)]
    dot_general x4, matrix products: 22.6 us -> 19.3 us  [take(): return jnp.dot(rows, matrix, preferred_element_type=f32)]
    ppermute x0 -> x3, starting transfers between devices: none -> 3.01 us  [per_device(): blocks = blocks + [lax.ppermute(block, 'tp', partners) for block in blocks]]
    unnamed x40 -> x48, local copies, waits for them, and re-layouts: 11.9 us -> 12.7 us
  transfers between devices with their start and end apart: 8 -> 10, of which waited for: 7 -> 6; matrix products, arithmetic and copies ran while one was open for 14% -> 14% of each run, Pallas kernels for 2% -> 2%
where the time goes in v3:
time: 223 us
  waiting for transfers between devices  105 us (47%)
  Pallas kernels  28.5 us (13%)
  local copies, waits for them, and re-layouts  19.8 us (9%)
  matrix products  19.3 us (9%)
  between operations  17.5 us (8%)
  other arithmetic  14.1 us (6%)
  starting transfers between devices  12.4 us (6%)
  blocking collectives  6.07 us (3%)
    ppermute x3, waiting for transfers between devices, per_device(): slots = own + lax.ppermute(sent, 'seq', partners)  39.3 us
    all_gather x1, waiting for transfers between devices, per_device(): pieces = lax.all_gather(end, 'seq')  38.6 us
    ppermute x3, waiting for transfers between devices, per_device(): blocks = blocks + [lax.ppermute(block, 'tp', partners) for block in blocks]  26.8 us
    dot_general x4, matrix products, take(): return jnp.dot(rows, matrix, preferred_element_type=f32)  19.3 us
    unnamed x48, local copies, waits for them, and re-layouts  12.7 us
    pallas_call x1, Pallas kernels, per_device(): pl.pallas_call(states_kernel, grid=(chunks,), in_specs=[smem, stepped((CH...  12.3 us
    pallas_call x1, Pallas kernels, per_device(): pl.pallas_call(finish_kernel, grid=(rows_here // wide,), in_specs=[smem,...  10.9 us
    psum x1, blocking collectives, per_device(): lax.psum(square.reshape(rows_here // LANES, LANES), 'tp')  6.07 us
  transfers between devices with their start and end apart: 10, of which 6 were waited for; matrix products, arithmetic and copies ran while one was open for 14% of the time, Pallas kernels for 2%

profile of v3, /device:TPU:0, one launch (start us, length us, event | category | flops | bytes accessed | tf_op | source)
XLA Modules:
  0.0 222.6 jit_solution(14557356507296553842)
XLA Ops:
  7.2 3.0 %collective-permute-start = (bf16[1024,512]{1,0:T(8,128)(2,1)}, bf16[1024,512]{1,0:T(8,128)(2,1)S(1)}, u32[]{:S(2)}, u32[]{:S(2)}) collective-permute-start(bf16[1024,512]{1,0:T(8,128)(2,1)} %param.14), channel_id=1, source_target_pairs={{0,2},{1,3},{2,0},{3,1},{4,6},{5,7},{6,4},{7,5},{8,10},{9,11},{10,... | collective-permute-start | bytes 3145736 | tf_op jit(solution)/shard_map/ppermute | solution.py:301
  12.5 26.8 %collective-permute-done = bf16[1024,512]{1,0:T(8,128)(2,1)S(1)} collective-permute-done((bf16[1024,512]{1,0:T(8,128)(2,1)}, bf16[1024,512]{1,0:T(8,128)(2,1)S(1)}, u32[]{:S(2)}, u32[]{:S(2)}) %collective-permute-start) | collective-permute-done | bytes 1048608 | tf_op jit(solution)/shard_map/ppermute | solution.py:301
  41.0 1.5 constant_dynamic-update-slice_fusion.1
  43.5 4.7 %convolution_convert_fusion.1.x_ref = bf16[1024,1024]{1,0:T(8,128)(2,1)S(1)} fusion(bf16[1024,2048]{1,0:T(8,128)(2,1)S(1)} %constant_dynamic-update-slice_fusion, bf16[2048,1024]{1,0:T(8,128)(2,1)S(1)} %copy-done.21), kind=kOutput, calls=%fused_computation.3 | convolution fusion | flops 4296015872 | bytes 10485760 | tf_op jit(solution)/shard_map/dot_general | solution.py:310
  48.2 1.3 copy-done.1
  49.5 3.9 %convolution_convert_fusion.2.bc_ref = bf16[1024,256]{1,0:T(8,128)(2,1)S(1)} fusion(bf16[1024,2048]{1,0:T(8,128)(2,1)} %copy-done.15, bf16[2048,256]{0,1:T(8,128)(2,1)} %all-gather.4.cloned.1.call-done), kind=kOutput, calls=%fused_computation.4 | convolution fusion | flops 1074003968 | bytes 5767168 | tf_op jit(solution)/shard_map/dot_general | solution.py:310
  53.5 3.8 %collective-permute-start.3 = (bf16[16,1280]{1,0:T(8,128)(2,1)S(1)}, bf16[16,1280]{1,0:T(8,128)(2,1)S(1)}, u32[]{:S(2)}, u32[]{:S(2)}) collective-permute-start(bf16[16,1280]{1,0:T(8,128)(2,1)S(1)} %pad_maximum_fusion), channel_id=1, source_target_pairs={{0,4},{4,8},{8,12},{12,16},{16,20},{20,24},{24,28},{1,5},{5,9},{9,... | collective-permute-start | bytes 122888 | tf_op jit(solution)/shard_map/ppermute | solution.py:315
  57.4 1.2 fusion.21.dt_ref
  59.1 12.3 %shard_map.165 = (bf16[1024,1024]{1,0:T(8,128)(2,1)S(1)}, bf16[1024,1024]{1,0:T(8,128)(2,1)S(1)}, bf16[1024,256]{1,0:T(8,128)(2,1)S(1)}, f32[1024,128]{1,0:T(8,1...) custom-call(s32[16]{0:T(128)S(1)} %pad_add_fusion.place_ref, ...), custom_call_target="tpu_custom_call" | custom-call | flops 8000000000 | bytes 16000000 | tf_op jit(solution)/shard_map/pallas_call | solution.py:324
  71.3 1.4 copy-done.7
  72.7 1.4 copy-done.10
  74.0 1.3 copy-done.12
  75.8 9.5 %convolution_convert_fusion.z_ref = bf16[1024,1024]{1,0:T(8,128)(2,1)} fusion(bf16[1024,2048]{1,0:T(8,128)(2,1)} %copy-done.15, bf16[2048,1024]{1,0:T(8,128)(2,1)} %param.16), kind=kOutput, calls=%fused_computation.2 | convolution fusion | flops 4296015872 | bytes 10485760 | tf_op jit(solution)/shard_map/dot_general | solution.py:310
  85.3 5.4 %shard_map.166.y_ref = f32[1024,1024]{1,0:T(8,128)S(1)} custom-call(s32[16]{0:T(128)S(1)} %pad_add_fusion.place_ref, bf16[1024,1024]{1,0:T(8,128)(2,1)S(1)} %copy-done.11, bf16[1024,1024]{1,0:T(8,128)(2,1)S(1)} %copy-done.13, bf16[1024,256]{1,0:T(8,128)(2,1)S(1)} %get-tuple-element.18.bcc_ref, f32[1024,128]{1,0:T(8,128)S(1)} %get-tuple-element.19.acum_ref, ...), custom_call_target="tpu_custom_call" | custom-call | flops 8000000000 | bytes 16000000 | tf_op jit(solution)/shard_map/pallas_call | solution.py:376
  90.7 1.9 copy-done.6
  92.6 38.6 %all-gather.6.cloned.1.call-done = bf16[1152,1024]{1,0:T(8,128)(2,1)} async-done(((bf16[144,1024]{1,0:T(8,128)(2,1)}), bf16[1152,1024]{1,0:T(8,128)(2,1)}) %all-gather.6.cloned.1.call-update) | async-done | bytes 2359312 | tf_op jit(solution)/shard_map/all_gather | solution.py:374
  131.1 1.1 fusion.34
  132.2 1.9 fusion.12.entering_ref
  134.1 1.6 copy-done.9
  135.7 10.9 %shard_map.167 = (bf16[4,1024,512]{2,1,0:T(8,128)(2,1)S(1)}, f32[1024,1]{1,0:T(8,128)S(1)}) custom-call(s32[16]{0:T(128)S(1)} %pad_add_fusion.place_ref, f32[1024,1024]{1,0:T(8,128)} %copy-done.6, bf16[1024,256]{1,0:T(8,128)(2,1)S(1)} %get-tuple-element.18.bcc_ref, f32[1024,128]{1,0:T(8,128)S(1)} %get-tuple-element.19.acum_ref, ...), custom_call_target="tpu_custom_call" | custom-call | flops 8000000000 | bytes 16000000 | tf_op jit(solution)/shard_map/pallas_call | solution.py:411
  146.6 1.9 copy-done
  150.0 1.3 select_select_fusion
  152.0 26.0 %collective-permute-done.4 = bf16[4,144,1024]{2,1,0:T(8,128)(2,1)S(1)} collective-permute-done((bf16[4,144,1024]{2,1,0:T(8,128)(2,1)}, bf16[4,144,1024]{2,1,0:T(8,128)(2,1)S(1)}, u32[]{:S(2)}, u32[]{:S(2)}) %collective-permute-start.4) | collective-permute-done | bytes 1179680 | tf_op jit(solution)/shard_map/ppermute | solution.py:468
  179.0 1.7 select_add_fusion
  180.8 1.7 collective-permute-start.5
  182.5 11.4 %collective-permute-done.5 = bf16[2,144,1024]{2,1,0:T(8,128)(2,1)S(1)} collective-permute-done((bf16[2,144,1024]{2,1,0:T(8,128)(2,1)S(1)}, bf16[2,144,1024]{2,1,0:T(8,128)(2,1)S(1)}, u32[]{:S(2)}, u32[]{:S(2)}) %collective-permute-start.5) | collective-permute-done | bytes 589856 | tf_op jit(solution)/shard_map/ppermute | solution.py:468
  194.7 3.0 %collective-permute-start.6 = (bf16[1,144,1024]{2,1,0:T(8,128)(2,1)}, bf16[1,144,1024]{2,1,0:T(8,128)(2,1)}, u32[]{:S(2)}, u32[]{:S(2)}) collective-permute-start(bf16[1,144,1024]{2,1,0:T(8,128)(2,1)} %select_bitcast_fusion.1), channel_id=1, source_target_pairs={{0,16},{4,20},{8,24},{12,28},{16,0},{20,4},{24,8},{28,12},{1,17},{... | collective-permute-start | bytes 884744 | tf_op jit(solution)/shard_map/ppermute | solution.py:468
  201.2 6.1 %psum.7 = f32[8,128]{1,0:T(8,128)S(1)} all-reduce(f32[8,128]{1,0:T(8,128)S(1)} %bitcast.156), channel_id=1, replica_groups=mesh['seq'=8,'tp'=4] {'tp'}, use_global_device_ids=true, to_apply=%region_2.3 | all-reduce | flops 1024 | bytes 8192 | tf_op jit(solution)/shard_map/psum | solution.py:444
  207.2 1.8 collective-permute-done.6
  209.0 1.0 bitcast_add_fusion.1
  212.3 1.3 slice_bitcast_fusion.14
  213.6 2.5 %fusion = bf16[1024,512]{1,0:T(8,128)(2,1)} fusion(bf16[1,1024,512]{2,1,0:T(8,128)(2,1)} %reduce-scatter.2.cloned.1.call-done, f32[1024]{0:T(1024)S(1)} %rsqrt_bitcast_fusion), kind=kLoop, calls=%fused_computation.1 | loop fusion | flops 1572864 | bytes 2101248 | tf_op jit(solution)/shard_map/convert_element_type | solution.py:445
  (93 shorter events, 12.2 us)
Async XLA Ops:
  7.2 33.2 %copy-start.19 = (bf16[1024,512]{1,0:T(8,128)(2,1)S(1)}, bf16[1024,512]{1,0:T(8,128)(2,1)}, u32[]{:S(2)}) copy-start(bf16[1024,512]{1,0:T(8,128)(2,1)} %param.14) | copy-start | bytes 3145732
  7.2 42.4 %all-gather.4.cloned.1.call-start = ((), (), s32[]{:S(2)}) async-start(), calls=%async_computation.1 | async-start | bytes 1310720 | tf_op jit(solution)/shard_map/all_gather | solution.py:294
  7.2 32.0 %collective-permute-start = (bf16[1024,512]{1,0:T(8,128)(2,1)}, bf16[1024,512]{1,0:T(8,128)(2,1)S(1)}, u32[]{:S(2)}, u32[]{:S(2)}) collective-permute-start(bf16[1024,512]{1,0:T(8,128)(2,1)} %param.14), channel_id=1, source_target_pairs={{0,2},{1,3},{2,0},{3,1},{4,6},{5,7},{6,4},{7,5},{8,10},{9,11},{10,... | collective-permute-start | bytes 3145736 | tf_op jit(solution)/shard_map/ppermute | solution.py:301
  10.2 30.8 %collective-permute-start.1 = (bf16[1024,512]{1,0:T(8,128)(2,1)}, bf16[1024,512]{1,0:T(8,128)(2,1)}, u32[]{:S(2)}, u32[]{:S(2)}) collective-permute-start(bf16[1024,512]{1,0:T(8,128)(2,1)} %param.14), channel_id=1, source_target_pairs={{0,1},{1,0},{2,3},{3,2},{4,5},{5,4},{6,7},{7,6},{8,9},{9,8},{10,11... | collective-permute-start | bytes 3145736 | tf_op jit(solution)/shard_map/ppermute | solution.py:301
  10.3 120.9 %all-gather.6.cloned.1.call-start = ((), (), s32[]{:S(2)}) async-start(), calls=%async_computation.3 | async-start | bytes 2654208 | tf_op jit(solution)/shard_map/all_gather | solution.py:374
  39.2 3.3 %collective-permute-start.2 = (bf16[1024,512]{1,0:T(8,128)(2,1)S(1)}, bf16[1024,512]{1,0:T(8,128)(2,1)S(1)}, u32[]{:S(2)}, u32[]{:S(2)}) collective-permute-start(bf16[1024,512]{1,0:T(8,128)(2,1)S(1)} %collective-permute-done), channel_id=1, source_target_pairs={{0,1},{1,0},{2,3},{3,2},{4,5},{5,4},{6,7},{7,6},{8,9},{9,8},{10,11... | collective-permute-start | bytes 3145736 | tf_op jit(solution)/shard_map/ppermute | solution.py:301
  41.0 2.5 %copy-start.21 = (bf16[2048,1024]{1,0:T(8,128)(2,1)S(1)}, bf16[2048,1024]{1,0:T(8,128)(2,1)}, u32[]{:S(2)}) copy-start(bf16[2048,1024]{1,0:T(8,128)(2,1)} %param.15) | copy-start | bytes 12582916
  43.5 4.7 %copy-start.15 = (bf16[1024,2048]{1,0:T(8,128)(2,1)}, bf16[1024,2048]{1,0:T(8,128)(2,1)S(1)}, u32[]{:S(2)}) copy-start(bf16[1024,2048]{1,0:T(8,128)(2,1)S(1)} %constant_dynamic-update-slice_fusion) | copy-start | bytes 12582916
  48.2 1.3 copy-start.1
  49.5 7.8 %copy-start.22 = (bf16[2048,16]{0,1:T(8,128)(2,1)S(1)}, bf16[2048,16]{0,1:T(8,128)(2,1)}, u32[]{:S(2)}) copy-start(bf16[2048,16]{0,1:T(8,128)(2,1)} %param.18) | copy-start | bytes 196612
  49.5 7.8 %copy-start.16 = (bf16[1024,2048]{1,0:T(8,128)(2,1)S(1)}, bf16[1024,2048]{1,0:T(8,128)(2,1)}, u32[]{:S(2)}) copy-start(bf16[1024,2048]{1,0:T(8,128)(2,1)} %copy-done.15) | copy-start | bytes 12582916
  53.5 5.5 %copy-start.2 = (bf16[1024,1024]{1,0:T(8,128)(2,1)S(1)}, bf16[1024,1024]{1,0:T(8,128)(2,1)}, u32[]{:S(2)}) copy-start(bf16[1024,1024]{1,0:T(8,128)(2,1)} %copy-done.1) | copy-start | bytes 6291460
  53.5 5.5 %copy-start.3 = (f32[4,1024]{1,0:T(4,128)S(1)}, f32[4,1024]{1,0:T(4,128)}, u32[]{:S(2)}) copy-start(f32[4,1024]{1,0:T(4,128)} %taps_x_ref.1) | copy-start | bytes 49156
  53.5 5.5 %copy-start.4 = (f32[4,256]{1,0:T(4,128)S(1)}, f32[4,256]{1,0:T(4,128)}, u32[]{:S(2)}) copy-start(f32[4,256]{1,0:T(4,128)} %taps_bc_ref.1) | copy-start | bytes 12292
  53.5 5.5 %collective-permute-start.3 = (bf16[16,1280]{1,0:T(8,128)(2,1)S(1)}, bf16[16,1280]{1,0:T(8,128)(2,1)S(1)}, u32[]{:S(2)}, u32[]{:S(2)}) collective-permute-start(bf16[16,1280]{1,0:T(8,128)(2,1)S(1)} %pad_maximum_fusion), channel_id=1, source_target_pairs={{0,4},{4,8},{8,12},{12,16},{16,20},{20,24},{24,28},{1,5},{5,9},{9,... | collective-permute-start | bytes 122888 | tf_op jit(solution)/shard_map/ppermute | solution.py:315
  59.0 16.6 %copy-start.20 = (f32[16]{0:T(128)S(1)}, f32[16]{0:T(128)}, u32[]{:S(2)}) copy-start(f32[16]{0:T(128)} %param.23) | copy-start | bytes 196
  71.3 1.4 copy-start.7
  72.7 1.4 copy-start.10
  74.0 1.3 copy-start.12
  75.4 138.2 %reduce-scatter.2.cloned.1.call-start = ((), (), s32[]{:S(2)}) async-start(), calls=%async_computation.2 | async-start | bytes 5242880 | tf_op jit(solution)/shard_map/reduce_scatter | solution.py:443
  75.8 9.5 %copy-start.11 = (bf16[1024,1024]{1,0:T(8,128)(2,1)S(1)}, bf16[1024,1024]{1,0:T(8,128)(2,1)}, u32[]{:S(2)}) copy-start(bf16[1024,1024]{1,0:T(8,128)(2,1)} %copy-done.10) | copy-start | bytes 6291460
  75.8 9.5 %copy-start.13 = (bf16[1024,1024]{1,0:T(8,128)(2,1)S(1)}, bf16[1024,1024]{1,0:T(8,128)(2,1)}, u32[]{:S(2)}) copy-start(bf16[1024,1024]{1,0:T(8,128)(2,1)} %copy-done.12) | copy-start | bytes 6291460
  90.7 1.9 copy-start.6
  92.6 41.5 %copy-start.5 = (f32[1024]{0:T(1024)S(1)}, f32[1024]{0:T(1024)}, u32[]{:S(2)}) copy-start(f32[1024]{0:T(1024)} %param.24) | copy-start | bytes 12292
  131.1 3.0 %copy-start.8 = (bf16[8,128,1024]{2,1,0:T(8,128)(2,1)S(1)}, bf16[8,128,1024]{2,1,0:T(8,128)(2,1)}, u32[]{:S(2)}) copy-start(bf16[8,128,1024]{2,1,0:T(8,128)(2,1)} %copy-done.7) | copy-start | bytes 6291460
  134.1 1.6 copy-start.9
  146.6 1.9 copy-start
  151.3 26.7 %collective-permute-start.4 = (bf16[4,144,1024]{2,1,0:T(8,128)(2,1)}, bf16[4,144,1024]{2,1,0:T(8,128)(2,1)S(1)}, u32[]{:S(2)}, u32[]{:S(2)}) collective-permute-start(bf16[4,144,1024]{2,1,0:T(8,128)(2,1)} %select_select_fusion), channel_id=1, source_target_pairs={{0,4},{4,0},{8,12},{12,8},{16,20},{20,16},{24,28},{28,24},{1,5},{5... | collective-permute-start | bytes 3538952 | tf_op jit(solution)/shard_map/ppermute | solution.py:468
  178.0 1.0 copy-start.17
  180.8 13.1 %collective-permute-start.5 = (bf16[2,144,1024]{2,1,0:T(8,128)(2,1)S(1)}, bf16[2,144,1024]{2,1,0:T(8,128)(2,1)S(1)}, u32[]{:S(2)}, u32[]{:S(2)}) collective-permute-start(bf16[2,144,1024]{2,1,0:T(8,128)(2,1)S(1)} %select_bitcast_fusion), channel_id=1, source_target_pairs={{0,8},{4,12},{8,0},{12,4},{16,24},{20,28},{24,16},{28,20},{1,9},{5... | collective-permute-start | bytes 1769480 | tf_op jit(solution)/shard_map/ppermute | solution.py:468
  194.0 16.8 %copy-start.14 = (bf16[1152,1024]{1,0:T(8,128)(2,1)S(1)}, bf16[1152,1024]{1,0:T(8,128)(2,1)}, u32[]{:S(2)}) copy-start(bf16[1152,1024]{1,0:T(8,128)(2,1)} %all-gather.6.cloned.1.call-done) | copy-start | bytes 7077892
  194.7 14.3 %collective-permute-start.6 = (bf16[1,144,1024]{2,1,0:T(8,128)(2,1)}, bf16[1,144,1024]{2,1,0:T(8,128)(2,1)}, u32[]{:S(2)}, u32[]{:S(2)}) collective-permute-start(bf16[1,144,1024]{2,1,0:T(8,128)(2,1)} %select_bitcast_fusion.1), channel_id=1, source_target_pairs={{0,16},{4,20},{8,24},{12,28},{16,0},{20,4},{24,8},{28,12},{1,17},{... | collective-permute-start | bytes 884744 | tf_op jit(solution)/shard_map/ppermute | solution.py:468
  (2 other events, 1.4 us)
Sparse Core Ops, SparseCore 0:
  10.4 24.3 all-gather.3
  75.5 55.6 all-gather.5
  148.7 43.0 reduce-scatter.1
